TPU v7x, 512 devices: a whole 4x8x8 slice. The times are simulated.
512 devices in a mesh: gx: 8 (over z), gy: 16 (over y_lo, x), gz: 4 (over y_hi, core).
Axes of the slice: x: 4, y: 8 (y_hi: 2, y_lo: 4; y = y_hi * 4 + y_lo), z: 8, core: 2. Of those that a mesh axis runs over, the one named last changes fastest.
Arguments:
- q_dagger: float32 [64, 128, 32, 512], P(None, 'gy', 'gx', 'gz'), may hold values from 0.2 to 3
- forward: float32 [2, 64, 128, 32, 512], P(None, None, 'gy', 'gx', 'gz'), may hold values from 0.2 to 2
- field_iso: float32 [128, 32, 512], P('gy', 'gx', 'gz'), may hold values from -6 to 6
- field_order: float32 [3, 128, 32, 512], P(None, 'gy', 'gx', 'gz'), may hold values from -6 to 6
- sphere_step: float32 [64, 64], replicated, may hold values from -0.75 to 0.75
- upwind_sign: int32 [3, 64], replicated, may hold values from 0 to 1, as said below
- direction_size: float32 [3, 64], replicated, may hold values from 0.1 to 1
- sphere_weight: float32 [64], replicated, may hold values from 0.05 to 0.3
Outputs:
- q_final: float32 [64, 128, 32, 512], P(None, 'gy', 'gx', 'gz')
- density: float32 [128, 32, 512], P('gy', 'gx', 'gz')
- order_density: float32 [3, 128, 32, 512], P(None, 'gy', 'gx', 'gz')
Inputs may be any that keep to these rules, and one draw needn't show every extreme that they name: `upwind_sign`: 1 marks an orientation whose upwind neighbour along that axis lies at the higher index, 0 at the lower; along each axis exactly 32 orientations are 1.
All inputs are finite; a program needn't handle non-finite values.
Results may differ from a plain program's by a relative error of at most 0.00017.
Values sent between devices are 32-bit elements; how exact they have to be, the bound alone decides.
A program may use at most 64 MiB of HBM per device.

v0:
```python
import jax
import jax.numpy as jnp
from jax import lax
from jax.sharding import PartitionSpec as P

STEPS = 2


SPEED = 0.5
HALF_DOSE = 0.2


def extended(cells, sides, width):
    for axis, dim in sides:
        count = lax.axis_size(axis)
        head = lax.slice_in_dim(cells, 0, width, axis=dim)
        tail = lax.slice_in_dim(cells, cells.shape[dim] - width, cells.shape[dim], axis=dim)
        cells = jnp.concatenate(
            [
                lax.ppermute(tail, axis, [(i, (i + 1) % count) for i in range(count)]),
                cells,
                lax.ppermute(head, axis, [((i + 1) % count, i) for i in range(count)]),
            ],
            axis=dim,
        )
    return cells


def directions(upwind_sign, direction_size):
    signed = (2 * upwind_sign - 1).astype(jnp.float32) * direction_size
    length = jnp.sqrt(jnp.sum(signed * signed, axis=0))
    return signed / length


def exponent_factor(field_iso, field_order, shape_terms):
    field = field_iso[None] + jnp.einsum(
        "au,axyz->uxyz", shape_terms, field_order, precision=lax.Precision.HIGHEST
    )
    return jnp.exp(-HALF_DOSE * field)


def advect_parts(center, uppers, lowers, along, upwind_sign):
    moved = center
    for direction_axis in range(3):
        upper_side = (upwind_sign[direction_axis] == 1)[:, None, None, None]
        speeds = jnp.abs(along[direction_axis])[:, None, None, None]
        chosen = jnp.where(upper_side, uppers[direction_axis], lowers[direction_axis])
        moved = moved + SPEED * speeds * (chosen - center)
    return moved


def advect(padded, along, upwind_sign):
    center = padded[:, 1:-1, 1:-1, 1:-1]
    uppers = (padded[:, 2:, 1:-1, 1:-1], padded[:, 1:-1, 2:, 1:-1], padded[:, 1:-1, 1:-1, 2:])
    lowers = (padded[:, :-2, 1:-1, 1:-1], padded[:, 1:-1, :-2, 1:-1], padded[:, 1:-1, 1:-1, :-2])
    return advect_parts(center, uppers, lowers, along, upwind_sign)


def sphere_mix(values, sphere_step):
    flat = values.reshape(values.shape[0], -1)
    mixed = jnp.dot(
        sphere_step, flat, precision=lax.Precision.HIGHEST, preferred_element_type=jnp.float32
    )
    return mixed.reshape(values.shape)


def accumulate(density, order_density, forward_slice, current, sphere_weight, shape_terms):
    product = sphere_weight[:, None, None, None] * forward_slice * current
    density = density + jnp.sum(product, axis=0) / STEPS
    order_density = (
        order_density
        + jnp.einsum("au,uxyz->axyz", shape_terms, product, precision=lax.Precision.HIGHEST) / STEPS
    )
    return (density, order_density)


def body(
    q_dagger,
    forward,
    field_iso,
    field_order,
    sphere_step,
    upwind_sign,
    direction_size,
    sphere_weight,
):
    along = directions(upwind_sign, direction_size)
    shape_terms = along * along - 1.0 / 3.0
    current = q_dagger
    density = jnp.zeros(field_iso.shape, jnp.float32)
    order_density = jnp.zeros(field_order.shape, jnp.float32)
    factor = exponent_factor(field_iso, field_order, shape_terms)
    for contour in range(STEPS):
        weighted = factor * current
        padded = extended(weighted, (("gx", 2), ("gy", 1), ("gz", 3)), 1)
        moved = advect(padded, along, upwind_sign)
        current = factor * sphere_mix(moved, sphere_step)
        density, order_density = accumulate(
            density, order_density, forward[contour], current, sphere_weight, shape_terms
        )
    return (current, density, order_density)


def solution(mesh):
    placed = (
        P(None, "gy", "gx", "gz"),
        P(None, None, "gy", "gx", "gz"),
        P("gy", "gx", "gz"),
        P(None, "gy", "gx", "gz"),
        P(),
        P(),
        P(),
        P(),
    )
    return jax.shard_map(
        body,
        mesh=mesh,
        in_specs=placed,
        out_specs=(P(None, "gy", "gx", "gz"), P("gy", "gx", "gz"), P(None, "gy", "gx", "gz")),
        check_vma=False,
    )
```

profile of v0, /device:TPU:1, one launch (start us, length us, event | category | flops | bytes accessed | tf_op | source)
XLA Modules:
  0.0 150.2 jit_solution(12307494795515870624)
XLA Ops:
  2.1 3.0 %copy_multiply_fusion.2 = (f32[64,8,4,128]{3,0,2,1:T(8,128)S(1)}, f32[64,8,4,128]{3,0,2,1:T(8,128)S(1)}) fusion(f32[64,8,4,128]{3,2,1,0:T(4,128)} %param.8, f32[3,8,4,128]{3,2,1,0:T(4,128)S(1)} %copy-done, f32[3,64]{1,0:T(4,128)S(1)} %broadcast_divide_fusion, f32[8,4,128]{2,1,0:T(4,128)} %param.10), kind=kOutput, calls=%fused_computation.77 | convolution fusion | flops 10224000 | bytes 3212032 | tf_op jit(solution)/shard_map/au,axyz->uxyz/dot_general | solution.py:36
  5.2 4.8 %collective-permute-start = (f32[64,8,1,128]{3,0,2,1:T(8,128)S(1)}, f32[64,8,1,128]{3,0,2,1:T(8,128)S(1)}, u32[]{:S(2)}, u32[]{:S(2)}) collective-permute-start(f32[64,8,1,128]{3,0,2,1:T(8,128)S(1)} %get-tuple-element.29), channel_id=1, source_target_pairs={{0,64},{64,128},{128,192},{192,256},{256,320},{320,384},{384,448},... | collective-permute-start | bytes 786440 | tf_op jit(solution)/shard_map/ppermute | solution.py:20
  10.0 8.6 %collective-permute-start.1 = (f32[64,8,1,128]{3,0,2,1:T(8,128)S(1)}, f32[64,8,1,128]{3,0,2,1:T(8,128)S(1)}, u32[]{:S(2)}, u32[]{:S(2)}) collective-permute-start(f32[64,8,1,128]{3,0,2,1:T(8,128)S(1)} %get-tuple-element.30), channel_id=1, source_target_pairs={{64,0},{128,64},{192,128},{256,192},{320,256},{384,320},{448,384},... | collective-permute-start | bytes 786440 | tf_op jit(solution)/shard_map/ppermute | solution.py:22
  19.8 2.9 %collective-permute-done = f32[64,8,1,128]{3,0,2,1:T(8,128)S(1)} collective-permute-done((f32[64,8,1,128]{3,0,2,1:T(8,128)S(1)}, f32[64,8,1,128]{3,0,2,1:T(8,128)S(1)}, u32[]{:S(2)}, u32[]{:S(2)}) %collective-permute-start) | collective-permute-done | bytes 262176 | tf_op jit(solution)/shard_map/ppermute | solution.py:20
  23.6 3.1 %collective-permute-start.3 = (f32[64,1,6,128]{3,0,2,1:T(8,128)S(1)}, f32[64,1,6,128]{3,0,2,1:T(8,128)S(1)}, u32[]{:S(2)}, u32[]{:S(2)}) collective-permute-start(f32[64,1,6,128]{3,0,2,1:T(8,128)S(1)} %get-tuple-element.25), channel_id=1, source_target_pairs={{0,4},{4,8},{8,12},{12,16},{16,20},{20,24},{24,28},{28,32},{32,36}... | collective-permute-start | bytes 589832 | tf_op jit(solution)/shard_map/ppermute | solution.py:20
  26.7 6.2 %collective-permute-start.2 = (f32[64,1,6,128]{3,0,2,1:T(8,128)S(1)}, f32[64,1,6,128]{3,0,2,1:T(8,128)S(1)}, u32[]{:S(2)}, u32[]{:S(2)}) collective-permute-start(f32[64,1,6,128]{3,0,2,1:T(8,128)S(1)} %get-tuple-element.26), channel_id=1, source_target_pairs={{4,0},{8,4},{12,8},{16,12},{20,16},{24,20},{28,24},{32,28},{36,32}... | collective-permute-start | bytes 589832 | tf_op jit(solution)/shard_map/ppermute | solution.py:22
  36.4 2.6 %fusion.49 = (f32[64,10,6,1]{3,0,2,1:T(8,128)}, f32[64,10,6,1]{3,0,2,1:T(8,128)}) fusion(f32[64,10,6,128]{3,0,2,1:T(8,128)S(1)} %pad_maximum_fusion), kind=kLoop, calls=%fused_computation.111 | loop fusion | bytes 61440 | tf_op jit(solution)/shard_map/slice | solution.py:16
  39.0 2.2 %copy.29 = f32[64,10,6,1]{0,3,2,1:T(1,128)S(1)} copy(f32[64,10,6,1]{3,0,2,1:T(8,128)} %get-tuple-element.21) | data formatting | bytes 30720 | tf_op jit(solution)/shard_map/slice | solution.py:16
  41.2 2.2 %copy.31 = f32[64,10,6,1]{0,3,2,1:T(1,128)S(1)} copy(f32[64,10,6,1]{3,0,2,1:T(8,128)} %get-tuple-element.22) | data formatting | bytes 30720 | tf_op jit(solution)/shard_map/slice | solution.py:17
  43.4 9.9 %collective-permute-start.5 = (f32[64,10,6,1]{0,3,2,1:T(1,128)S(1)}, f32[64,10,6,1]{0,3,2,1:T(1,128)S(1)}, u32[]{:S(2)}, u32[]{:S(2)}) collective-permute-start(f32[64,10,6,1]{0,3,2,1:T(1,128)S(1)} %copy.31), channel_id=1, source_target_pairs={{0,1},{1,2},{2,3},{3,0},{4,5},{5,6},{6,7},{7,4},{8,9},{9,10},{10,1... | collective-permute-start | bytes 46088 | tf_op jit(solution)/shard_map/ppermute | solution.py:20
  53.2 1.9 %collective-permute-start.4 = (f32[64,10,6,1]{0,3,2,1:T(1,128)S(1)}, f32[64,10,6,1]{0,3,2,1:T(1,128)}, u32[]{:S(2)}, u32[]{:S(2)}) collective-permute-start(f32[64,10,6,1]{0,3,2,1:T(1,128)S(1)} %copy.29), channel_id=1, source_target_pairs={{1,0},{2,1},{3,2},{0,3},{5,4},{6,5},{7,6},{4,7},{9,8},{10,9},{11,1... | collective-permute-start | bytes 46088 | tf_op jit(solution)/shard_map/ppermute | solution.py:22
  56.5 5.9 %collective-permute-done.4 = f32[64,10,6,1]{0,3,2,1:T(1,128)} collective-permute-done((f32[64,10,6,1]{0,3,2,1:T(1,128)S(1)}, f32[64,10,6,1]{0,3,2,1:T(1,128)}, u32[]{:S(2)}, u32[]{:S(2)}) %collective-permute-start.4) | collective-permute-done | bytes 15392 | tf_op jit(solution)/shard_map/ppermute | solution.py:22
  62.5 2.7 %copy.30 = f32[64,10,6,1]{3,0,2,1:T(8,128)} copy(f32[64,10,6,1]{0,3,2,1:T(1,128)} %collective-permute-done.4) | data formatting | bytes 30720 | tf_op jit(solution)/shard_map/ppermute | solution.py:22
  65.2 2.0 %copy.32 = f32[64,10,6,1]{3,0,2,1:T(8,128)} copy(f32[64,10,6,1]{0,3,2,1:T(1,128)S(1)} %collective-permute-done.5) | data formatting | bytes 30720 | tf_op jit(solution)/shard_map/ppermute | solution.py:20
  67.2 3.2 %fusion.18 = f32[64,8,4,128]{3,0,2,1:T(8,128)S(1)} fusion(f32[64,8,4,128]{3,0,2,1:T(8,128)S(1)} %get-tuple-element.37, f32[64,10,6,1]{3,0,2,1:T(8,128)} %copy.32, f32[64,1,6,128]{3,0,2,1:T(8,128)} %copy-done.6, f32[64,1,6,128]{3,0,2,1:T(8,128)} %copy-done.4, f32[64,8,1,128]{3,0,2,1:T(8,128)} %copy-done.1, f32[64,8,1,128]{3,0,2,1:T(8,128)S(1)} %collective-permute-done, ...), kind=kLoop, calls=%fused_computation.43 | loop fusion | flops 7864320 | bytes 3046336 | tf_op jit(solution)/shard_map/add | solution.py:48
  72.5 2.3 %convolution_bitcast_fusion.1 = f32[64,4096]{1,0:T(8,128)S(1)} fusion(f32[64,4096]{1,0:T(8,128)} %reshape.74, f32[64,64]{1,0:T(8,128)S(1)} %copy-done.8), kind=kOutput, calls=%fused_computation.1 | convolution fusion | flops 201326592 | bytes 2113536 | tf_op jit(solution)/shard_map/dot_general | solution.py:61
  76.5 4.4 %fusion.45 = (f32[8,4,128]{2,1,0:T(4,128)}, f32[64,8,4,128]{3,0,2,1:T(8,128)}, f32[64,8,4,128]{3,0,2,1:T(8,128)S(1)}) fusion(f32[64,8,4,128]{3,0,2,1:T(8,128)S(1)} %get-tuple-element.38, f32[64,8,4,128]{3,2,1,0:T(4,128)} %reshape.75, f32[1,64,8,4,128]{4,3,2,1,0:T(4,128)} %get-tuple-element.17, f32[64]{0:T(128)S(1)} %copy-done.18), kind=kLoop, calls=%fused_computation.108 | loop fusion | flops 1306624 | bytes 5259520 | tf_op jit(solution)/shard_map/reduce_sum | solution.py:69
  80.9 1.9 %collective-permute-start.6 = (f32[64,8,1,128]{3,0,2,1:T(8,128)S(1)}, f32[64,8,1,128]{3,0,2,1:T(8,128)S(1)}, u32[]{:S(2)}, u32[]{:S(2)}) collective-permute-start(f32[64,8,1,128]{3,0,2,1:T(8,128)S(1)} %get-tuple-element.27), channel_id=1, source_target_pairs={{0,64},{64,128},{128,192},{192,256},{256,320},{320,384},{384,448},... | collective-permute-start | bytes 786440 | tf_op jit(solution)/shard_map/ppermute | solution.py:20
  82.9 5.3 %collective-permute-start.7 = (f32[64,8,1,128]{3,0,2,1:T(8,128)S(1)}, f32[64,8,1,128]{3,0,2,1:T(8,128)S(1)}, u32[]{:S(2)}, u32[]{:S(2)}) collective-permute-start(f32[64,8,1,128]{3,0,2,1:T(8,128)S(1)} %get-tuple-element.28), channel_id=1, source_target_pairs={{64,0},{128,64},{192,128},{256,192},{320,256},{384,320},{448,384},... | collective-permute-start | bytes 786440 | tf_op jit(solution)/shard_map/ppermute | solution.py:22
  91.5 1.9 %collective-permute-start.9 = (f32[64,1,6,128]{3,0,2,1:T(8,128)S(1)}, f32[64,1,6,128]{3,0,2,1:T(8,128)S(1)}, u32[]{:S(2)}, u32[]{:S(2)}) collective-permute-start(f32[64,1,6,128]{3,0,2,1:T(8,128)S(1)} %get-tuple-element.23), channel_id=1, source_target_pairs={{0,4},{4,8},{8,12},{12,16},{16,20},{20,24},{24,28},{28,32},{32,36}... | collective-permute-start | bytes 589832 | tf_op jit(solution)/shard_map/ppermute | solution.py:20
  93.5 8.0 %collective-permute-start.8 = (f32[64,1,6,128]{3,0,2,1:T(8,128)S(1)}, f32[64,1,6,128]{3,0,2,1:T(8,128)S(1)}, u32[]{:S(2)}, u32[]{:S(2)}) collective-permute-start(f32[64,1,6,128]{3,0,2,1:T(8,128)S(1)} %get-tuple-element.24), channel_id=1, source_target_pairs={{4,0},{8,4},{12,8},{16,12},{20,16},{24,20},{28,24},{32,28},{36,32}... | collective-permute-start | bytes 589832 | tf_op jit(solution)/shard_map/ppermute | solution.py:22
  104.9 2.6 %fusion.48 = (f32[64,10,6,1]{3,0,2,1:T(8,128)}, f32[64,10,6,1]{3,0,2,1:T(8,128)}) fusion(f32[64,10,6,128]{3,0,2,1:T(8,128)S(1)} %pad_maximum_fusion.1), kind=kLoop, calls=%fused_computation.110 | loop fusion | bytes 61440 | tf_op jit(solution)/shard_map/slice | solution.py:16
  107.5 2.8 %copy.35 = f32[64,10,6,1]{0,3,2,1:T(1,128)} copy(f32[64,10,6,1]{3,0,2,1:T(8,128)} %get-tuple-element.19) | data formatting | bytes 30720 | tf_op jit(solution)/shard_map/slice | solution.py:16
  110.3 2.8 %copy.37 = f32[64,10,6,1]{0,3,2,1:T(1,128)} copy(f32[64,10,6,1]{3,0,2,1:T(8,128)} %get-tuple-element.20) | data formatting | bytes 30720 | tf_op jit(solution)/shard_map/slice | solution.py:17
  113.1 6.3 %collective-permute-start.11 = (f32[64,10,6,1]{0,3,2,1:T(1,128)}, f32[64,10,6,1]{0,3,2,1:T(1,128)}, u32[]{:S(2)}, u32[]{:S(2)}) collective-permute-start(f32[64,10,6,1]{0,3,2,1:T(1,128)} %copy.37), channel_id=1, source_target_pairs={{0,1},{1,2},{2,3},{3,0},{4,5},{5,6},{6,7},{7,4},{8,9},{9,10},{10,1... | collective-permute-start | bytes 46088 | tf_op jit(solution)/shard_map/ppermute | solution.py:20
  119.4 1.9 %collective-permute-start.10 = (f32[64,10,6,1]{0,3,2,1:T(1,128)}, f32[64,10,6,1]{0,3,2,1:T(1,128)}, u32[]{:S(2)}, u32[]{:S(2)}) collective-permute-start(f32[64,10,6,1]{0,3,2,1:T(1,128)} %copy.35), channel_id=1, source_target_pairs={{1,0},{2,1},{3,2},{0,3},{5,4},{6,5},{7,6},{4,7},{9,8},{10,9},{11,1... | collective-permute-start | bytes 46088 | tf_op jit(solution)/shard_map/ppermute | solution.py:22
  123.2 5.7 %collective-permute-done.10 = f32[64,10,6,1]{0,3,2,1:T(1,128)} collective-permute-done((f32[64,10,6,1]{0,3,2,1:T(1,128)}, f32[64,10,6,1]{0,3,2,1:T(1,128)}, u32[]{:S(2)}, u32[]{:S(2)}) %collective-permute-start.10) | collective-permute-done | bytes 15392 | tf_op jit(solution)/shard_map/ppermute | solution.py:22
  128.9 2.7 %copy.36 = f32[64,10,6,1]{3,0,2,1:T(8,128)} copy(f32[64,10,6,1]{0,3,2,1:T(1,128)} %collective-permute-done.10) | data formatting | bytes 30720 | tf_op jit(solution)/shard_map/ppermute | solution.py:22
  131.6 2.7 %copy.38 = f32[64,10,6,1]{3,0,2,1:T(8,128)} copy(f32[64,10,6,1]{0,3,2,1:T(1,128)} %collective-permute-done.11) | data formatting | bytes 30720 | tf_op jit(solution)/shard_map/ppermute | solution.py:20
  134.3 3.3 %fusion.6 = f32[64,8,4,128]{3,0,2,1:T(8,128)S(1)} fusion(f32[64,8,4,128]{3,0,2,1:T(8,128)S(1)} %get-tuple-element.16, f32[64,10,6,1]{3,0,2,1:T(8,128)} %copy.38, f32[64,1,6,128]{3,0,2,1:T(8,128)} %copy-done.7, f32[64,1,6,128]{3,0,2,1:T(8,128)} %copy-done.5, f32[64,8,1,128]{3,0,2,1:T(8,128)} %copy-done.2, f32[64,8,1,128]{3,0,2,1:T(8,128)S(1)} %collective-permute-done.6, ...), kind=kLoop, calls=%fused_computation.13 | loop fusion | flops 7864320 | bytes 3046336 | tf_op jit(solution)/shard_map/add | solution.py:48
  139.6 3.3 %convolution_bitcast_fusion = f32[64,4096]{1,0:T(8,128)} fusion(f32[64,4096]{1,0:T(8,128)} %reshape.76, f32[64,64]{1,0:T(8,128)S(1)} %copy-done.8), kind=kOutput, calls=%fused_computation | convolution fusion | flops 201326592 | bytes 2113536 | tf_op jit(solution)/shard_map/dot_general | solution.py:61
  142.9 1.9 %reshape.77 = f32[64,8,4,128]{3,2,1,0:T(4,128)S(1)} reshape(f32[64,4096]{1,0:T(8,128)} %convolution_bitcast_fusion) | data formatting | bytes 2097152 | tf_op jit(solution)/shard_map/reshape | solution.py:64
  (72 shorter events, 28.2 us)
Async XLA Ops:
  0.6 1.5 copy-start
  2.1 30.8 %copy-start.10 = (f32[3,64]{1,0:T(4,128)}, f32[3,64]{1,0:T(4,128)S(1)}, u32[]{:S(2)}) copy-start(f32[3,64]{1,0:T(4,128)S(1)} %broadcast_divide_fusion) | copy-start | bytes 2308
  2.1 16.5 %copy-start.3 = (f32[2,64,8,4,128]{4,3,2,1,0:T(4,128)S(1)}, f32[2,64,8,4,128]{4,3,2,1,0:T(4,128)}, u32[]{:S(2)}) copy-start(f32[2,64,8,4,128]{4,3,2,1,0:T(4,128)} %param.9) | copy-start | bytes 6291460
  5.2 17.5 %collective-permute-start = (f32[64,8,1,128]{3,0,2,1:T(8,128)S(1)}, f32[64,8,1,128]{3,0,2,1:T(8,128)S(1)}, u32[]{:S(2)}, u32[]{:S(2)}) collective-permute-start(f32[64,8,1,128]{3,0,2,1:T(8,128)S(1)} %get-tuple-element.29), channel_id=1, source_target_pairs={{0,64},{64,128},{128,192},{192,256},{256,320},{320,384},{384,448},... | collective-permute-start | bytes 786440 | tf_op jit(solution)/shard_map/ppermute | solution.py:20
  10.0 13.5 %collective-permute-start.1 = (f32[64,8,1,128]{3,0,2,1:T(8,128)S(1)}, f32[64,8,1,128]{3,0,2,1:T(8,128)S(1)}, u32[]{:S(2)}, u32[]{:S(2)}) collective-permute-start(f32[64,8,1,128]{3,0,2,1:T(8,128)S(1)} %get-tuple-element.30), channel_id=1, source_target_pairs={{64,0},{128,64},{192,128},{256,192},{320,256},{384,320},{448,384},... | collective-permute-start | bytes 786440 | tf_op jit(solution)/shard_map/ppermute | solution.py:22
  23.6 12.0 %copy-start.1 = (f32[64,8,1,128]{3,0,2,1:T(8,128)}, f32[64,8,1,128]{3,0,2,1:T(8,128)S(1)}, u32[]{:S(2)}) copy-start(f32[64,8,1,128]{3,0,2,1:T(8,128)S(1)} %collective-permute-done.1) | copy-start | bytes 786436
  23.6 10.9 %collective-permute-start.3 = (f32[64,1,6,128]{3,0,2,1:T(8,128)S(1)}, f32[64,1,6,128]{3,0,2,1:T(8,128)S(1)}, u32[]{:S(2)}, u32[]{:S(2)}) collective-permute-start(f32[64,1,6,128]{3,0,2,1:T(8,128)S(1)} %get-tuple-element.25), channel_id=1, source_target_pairs={{0,4},{4,8},{8,12},{12,16},{16,20},{20,24},{24,28},{28,32},{32,36}... | collective-permute-start | bytes 589832 | tf_op jit(solution)/shard_map/ppermute | solution.py:20
  26.7 8.8 %collective-permute-start.2 = (f32[64,1,6,128]{3,0,2,1:T(8,128)S(1)}, f32[64,1,6,128]{3,0,2,1:T(8,128)S(1)}, u32[]{:S(2)}, u32[]{:S(2)}) collective-permute-start(f32[64,1,6,128]{3,0,2,1:T(8,128)S(1)} %get-tuple-element.26), channel_id=1, source_target_pairs={{4,0},{8,4},{12,8},{16,12},{20,16},{24,20},{28,24},{32,28},{36,32}... | collective-permute-start | bytes 589832 | tf_op jit(solution)/shard_map/ppermute | solution.py:22
  34.5 1.0 copy-start.4
  35.5 0.7 copy-start.6
  43.4 21.8 %collective-permute-start.5 = (f32[64,10,6,1]{0,3,2,1:T(1,128)S(1)}, f32[64,10,6,1]{0,3,2,1:T(1,128)S(1)}, u32[]{:S(2)}, u32[]{:S(2)}) collective-permute-start(f32[64,10,6,1]{0,3,2,1:T(1,128)S(1)} %copy.31), channel_id=1, source_target_pairs={{0,1},{1,2},{2,3},{3,0},{4,5},{5,6},{6,7},{7,4},{8,9},{9,10},{10,1... | collective-permute-start | bytes 46088 | tf_op jit(solution)/shard_map/ppermute | solution.py:20
  53.2 9.2 %collective-permute-start.4 = (f32[64,10,6,1]{0,3,2,1:T(1,128)S(1)}, f32[64,10,6,1]{0,3,2,1:T(1,128)}, u32[]{:S(2)}, u32[]{:S(2)}) collective-permute-start(f32[64,10,6,1]{0,3,2,1:T(1,128)S(1)} %copy.29), channel_id=1, source_target_pairs={{1,0},{2,1},{3,2},{0,3},{5,4},{6,5},{7,6},{4,7},{9,8},{10,9},{11,1... | collective-permute-start | bytes 46088 | tf_op jit(solution)/shard_map/ppermute | solution.py:22
  62.5 4.7 %copy-start.12 = (f32[64]{0:T(128)S(1)}, f32[64]{0:T(128)}, u32[]{:S(2)}) copy-start(f32[64]{0:T(128)} %get-tuple-element.34) | copy-start | bytes 772
  62.5 4.7 %copy-start.13 = (f32[64]{0:T(128)S(1)}, f32[64]{0:T(128)}, u32[]{:S(2)}) copy-start(f32[64]{0:T(128)} %get-tuple-element.35) | copy-start | bytes 772
  62.5 4.7 %copy-start.14 = (f32[64]{0:T(128)S(1)}, f32[64]{0:T(128)}, u32[]{:S(2)}) copy-start(f32[64]{0:T(128)} %get-tuple-element.36) | copy-start | bytes 772
  62.5 4.7 %copy-start.15 = (pred[64]{0:T(512)(128)(4,1)S(1)}, pred[64]{0:T(512)(128)(4,1)}, u32[]{:S(2)}) copy-start(pred[64]{0:T(512)(128)(4,1)} %get-tuple-element.31) | copy-start | bytes 196
  62.5 4.7 %copy-start.16 = (pred[64]{0:T(512)(128)(4,1)S(1)}, pred[64]{0:T(512)(128)(4,1)}, u32[]{:S(2)}) copy-start(pred[64]{0:T(512)(128)(4,1)} %get-tuple-element.32) | copy-start | bytes 196
  62.5 4.7 %copy-start.17 = (pred[64]{0:T(512)(128)(4,1)S(1)}, pred[64]{0:T(512)(128)(4,1)}, u32[]{:S(2)}) copy-start(pred[64]{0:T(512)(128)(4,1)} %get-tuple-element.33) | copy-start | bytes 196
  70.4 2.1 %copy-start.8 = (f32[64,64]{1,0:T(8,128)S(1)}, f32[64,64]{1,0:T(8,128)}, u32[]{:S(2)}) copy-start(f32[64,64]{1,0:T(8,128)} %param.12) | copy-start | bytes 49156
  72.5 4.0 %copy-start.18 = (f32[64]{0:T(128)S(1)}, f32[64]{0:T(128)}, u32[]{:S(2)}) copy-start(f32[64]{0:T(128)} %param.15) | copy-start | bytes 772
  80.9 9.1 %collective-permute-start.6 = (f32[64,8,1,128]{3,0,2,1:T(8,128)S(1)}, f32[64,8,1,128]{3,0,2,1:T(8,128)S(1)}, u32[]{:S(2)}, u32[]{:S(2)}) collective-permute-start(f32[64,8,1,128]{3,0,2,1:T(8,128)S(1)} %get-tuple-element.27), channel_id=1, source_target_pairs={{0,64},{64,128},{128,192},{192,256},{256,320},{320,384},{384,448},... | collective-permute-start | bytes 786440 | tf_op jit(solution)/shard_map/ppermute | solution.py:20
  82.9 8.6 %collective-permute-start.7 = (f32[64,8,1,128]{3,0,2,1:T(8,128)S(1)}, f32[64,8,1,128]{3,0,2,1:T(8,128)S(1)}, u32[]{:S(2)}, u32[]{:S(2)}) collective-permute-start(f32[64,8,1,128]{3,0,2,1:T(8,128)S(1)} %get-tuple-element.28), channel_id=1, source_target_pairs={{64,0},{128,64},{192,128},{256,192},{320,256},{384,320},{448,384},... | collective-permute-start | bytes 786440 | tf_op jit(solution)/shard_map/ppermute | solution.py:22
  91.5 12.6 %copy-start.2 = (f32[64,8,1,128]{3,0,2,1:T(8,128)}, f32[64,8,1,128]{3,0,2,1:T(8,128)S(1)}, u32[]{:S(2)}) copy-start(f32[64,8,1,128]{3,0,2,1:T(8,128)S(1)} %collective-permute-done.7) | copy-start | bytes 786436
  91.5 11.1 %collective-permute-start.9 = (f32[64,1,6,128]{3,0,2,1:T(8,128)S(1)}, f32[64,1,6,128]{3,0,2,1:T(8,128)S(1)}, u32[]{:S(2)}, u32[]{:S(2)}) collective-permute-start(f32[64,1,6,128]{3,0,2,1:T(8,128)S(1)} %get-tuple-element.23), channel_id=1, source_target_pairs={{0,4},{4,8},{8,12},{12,16},{16,20},{20,24},{24,28},{28,32},{32,36}... | collective-permute-start | bytes 589832 | tf_op jit(solution)/shard_map/ppermute | solution.py:20
  93.5 10.6 %collective-permute-start.8 = (f32[64,1,6,128]{3,0,2,1:T(8,128)S(1)}, f32[64,1,6,128]{3,0,2,1:T(8,128)S(1)}, u32[]{:S(2)}, u32[]{:S(2)}) collective-permute-start(f32[64,1,6,128]{3,0,2,1:T(8,128)S(1)} %get-tuple-element.24), channel_id=1, source_target_pairs={{4,0},{8,4},{12,8},{16,12},{20,16},{24,20},{28,24},{32,28},{36,32}... | collective-permute-start | bytes 589832 | tf_op jit(solution)/shard_map/ppermute | solution.py:22
  102.6 1.5 copy-start.5
  104.1 0.7 copy-start.7
  113.1 18.5 %collective-permute-start.11 = (f32[64,10,6,1]{0,3,2,1:T(1,128)}, f32[64,10,6,1]{0,3,2,1:T(1,128)}, u32[]{:S(2)}, u32[]{:S(2)}) collective-permute-start(f32[64,10,6,1]{0,3,2,1:T(1,128)} %copy.37), channel_id=1, source_target_pairs={{0,1},{1,2},{2,3},{3,0},{4,5},{5,6},{6,7},{7,4},{8,9},{9,10},{10,1... | collective-permute-start | bytes 46088 | tf_op jit(solution)/shard_map/ppermute | solution.py:20
  119.4 9.4 %collective-permute-start.10 = (f32[64,10,6,1]{0,3,2,1:T(1,128)}, f32[64,10,6,1]{0,3,2,1:T(1,128)}, u32[]{:S(2)}, u32[]{:S(2)}) collective-permute-start(f32[64,10,6,1]{0,3,2,1:T(1,128)} %copy.35), channel_id=1, source_target_pairs={{1,0},{2,1},{3,2},{0,3},{5,4},{6,5},{7,6},{4,7},{9,8},{10,9},{11,1... | collective-permute-start | bytes 46088 | tf_op jit(solution)/shard_map/ppermute | solution.py:22
  139.6 5.2 %copy-start.19 = (f32[64]{0:T(128)S(1)}, f32[64]{0:T(128)}, u32[]{:S(2)}) copy-start(f32[64]{0:T(128)} %param.15) | copy-start | bytes 772
  146.1 1.7 %copy-start.11 = (f32[3,64]{1,0:T(4,128)S(1)}, f32[3,64]{1,0:T(4,128)}, u32[]{:S(2)}) copy-start(f32[3,64]{1,0:T(4,128)} %copy-done.10) | copy-start | bytes 2308
  146.1 3.5 %copy-start.9 = (f32[8,4,128]{2,1,0:T(4,128)S(1)}, f32[8,4,128]{2,1,0:T(4,128)}, u32[]{:S(2)}) copy-start(f32[8,4,128]{2,1,0:T(4,128)} %get-tuple-element.14) | copy-start | bytes 49156
where the time goes:
time: 151 us; the launch traced here: 150 us
  starting transfers between devices  60 us (40%)
  local copies, waits for them, and re-layouts  38 us (25%)
  waiting for transfers between devices  23.3 us (15%)
  other arithmetic  16.3 us (11%)
  matrix products  11.7 us (8%)
    ppermute x6, starting transfers between devices, extended(): lax.ppermute(head, axis, [((i + 1) % count, i) for i in range(count)])  32 us
    ppermute x6, starting transfers between devices, extended(): lax.ppermute(tail, axis, [(i, (i + 1) % count) for i in range(count)])  28 us
    ppermute x6, waiting for transfers between devices, extended(): lax.ppermute(head, axis, [((i + 1) % count, i) for i in range(count)])  16.4 us
    slice x4, local copies, waits for them, and re-layouts, extended(): head = lax.slice_in_dim(cells, 0, width, axis=dim)  10.2 us
    ppermute x6, waiting for transfers between devices, extended(): lax.ppermute(tail, axis, [(i, (i + 1) % count) for i in range(count)])  6.87 us
    add x2, other arithmetic, advect_parts(): moved = moved + SPEED * speeds * (chosen - center)  6.43 us
    dot_general x2, matrix products, sphere_mix(): jnp.dot(sphere_step, flat, precision=lax.Precision.HIGHEST, preferred_ele...  5.59 us
    reduce_sum x2, other arithmetic, accumulate(): density = density + jnp.sum(product, axis=0) / STEPS  5.58 us
  transfers between devices with their start and end apart: 12, of which 10 were waited for; matrix products, arithmetic and copies ran while one was open for 7% of the time, Pallas kernels for 0%

commit v1 on v0

v1 whole, which is shorter than its diff:
```python
import functools
import math

import jax
import jax.numpy as jnp
from jax import lax
from jax.experimental import pallas as pl
from jax.experimental.pallas import tpu as pltpu
from jax.sharding import PartitionSpec as P

U = 64
HALF = U // 2
LANES = 128
X = 8
Y = 4
ROWS = X * Y
STEPS = 2
RATE = -0.2 / math.log(2.0)
F32 = jnp.float32
BF16 = jnp.bfloat16

UP_X, LOW_X, UP_Y, LOW_Y, SPEED_Z, KEEP, SHAPE_0, SHAPE_1, SHAPE_2, SIGN_Z, RANK_X, RANK_Y = range(12)


def split(values):
    high = values.astype(BF16)
    low = (values - high.astype(F32)).astype(BF16)
    return high, low


def iota(shape, dim):
    return lax.broadcasted_iota(jnp.int32, shape, dim)


def neighbour(axis, step):
    count = lax.axis_size(axis)
    return {axis: lax.rem(lax.axis_index(axis) + count + step, count)}


def kernel(
    q_hbm, forward_hbm, iso_hbm, order_hbm, sphere_hbm, sign_hbm, size_hbm, weight_hbm,
    out_q, out_density, out_order,
    q, forward, factor, field, order, sphere, sign, size, weight,
    cells, coef, table, mix4, sum4, pack, unpack,
    send_x, send_y, send_z, recv_x, recv_y, recv_z, dens,
    load_sem, q_sem, forward_sem, store_sem, send_sem, recv_sem,
):
    sides = [("gx", 1), ("gx", -1), ("gy", 1), ("gy", -1), ("gz", 1), ("gz", -1)]
    barrier = pltpu.get_barrier_semaphore()
    for axis, step in sides:
        pl.semaphore_signal(
            barrier, inc=1, device_id=neighbour(axis, step), device_id_type=pl.DeviceIdType.MESH
        )

    small = [
        pltpu.make_async_copy(src, dst, load_sem.at[n])
        for n, (src, dst) in enumerate(
            [(sign_hbm, sign), (size_hbm, size), (weight_hbm, weight), (sphere_hbm, sphere),
             (iso_hbm, field), (order_hbm, order)]
        )
    ]
    for copy in small:
        copy.start()

    def load_q(row, carry):
        pltpu.make_async_copy(q_hbm.at[:, row, 0, :], q.at[row], q_sem.at[0]).start()
        return carry

    lax.fori_loop(0, ROWS, load_q, 0)

    def load_forward(row, carry):
        for step in range(STEPS):
            pltpu.make_async_copy(
                forward_hbm.at[step, :, row, 0, :], forward.at[step, row], forward_sem.at[step]
            ).start()
        return carry

    lax.fori_loop(0, ROWS, load_forward, 0)

    for copy in small:
        copy.wait()
    signs = sign[...].astype(F32)
    signed = (2.0 * signs - 1.0) * size[...]
    length = jnp.sqrt(jnp.sum(signed * signed, axis=0, keepdims=True))
    along = signed / length
    shape = along * along - 1.0 / 3.0
    speed = 0.5 * jnp.abs(along)
    below = (iota((U, U), 0) < iota((U, U), 1)).astype(BF16)
    ones_before = jnp.dot(signs.astype(BF16), below, preferred_element_type=F32)
    place = iota((1, U), 1).astype(F32)
    rank = jnp.where(signs > 0.5, ones_before, HALF + place - ones_before)
    keep = 1.0 - jnp.sum(speed, axis=0, keepdims=True)
    upper = speed * signs
    lower = speed * (1.0 - signs)
    rows = [
        upper[0:1], lower[0:1], upper[1:2], lower[1:2], speed[2:3], keep,
        RATE * shape[0:1], RATE * shape[1:2], RATE * shape[2:3],
        signs[2:3], rank[0:1], rank[1:2],
    ]
    stacked = jnp.zeros((16, U), F32)
    which = iota((16, U), 0)
    for n, row in enumerate(rows):
        stacked = jnp.where(which == n, row, stacked)
    table[...] = jnp.zeros((LANES, LANES), F32)
    table[0:16, 0:U] = stacked
    columns = jnp.transpose(table[...])
    for n in range(10):
        coef[n] = jnp.broadcast_to(columns[0:U, n : n + 1], (U, LANES))
    half_weight = weight[...] / STEPS
    sums = jnp.zeros((16, U), F32)
    for n, row in enumerate(
        [half_weight, half_weight * shape[0:1], half_weight * shape[1:2], half_weight * shape[2:3]]
    ):
        sums = jnp.where(which == n, row, sums)
    high, low = split(sums)
    sum4[...] = jnp.concatenate([high, high, low, low], axis=1)
    high, low = split(sphere[...])
    mix4[...] = jnp.concatenate([high, high, low, low], axis=1)
    for axis in range(2):
        to_rank = (iota((U, U), 0).astype(F32) == rank[axis : axis + 1]).astype(BF16)
        pack[axis] = jnp.concatenate([to_rank, to_rank], axis=1)
        from_rank = (
            iota((U, LANES), 1).astype(F32) == columns[0:U, RANK_X + axis : RANK_X + axis + 1]
        ) | (
            (iota((U, LANES), 1) - U).astype(F32) == columns[0:U, RANK_X + axis : RANK_X + axis + 1]
        )
        unpack[axis] = from_rank.astype(BF16)

    lane = iota((16, LANES), 1)

    pltpu.make_async_copy(q, q, q_sem.at[0]).wait()

    def start(x, carry):
        for group in range(4):
            part = pl.ds(16 * group, 16)
            shapes = [coef[SHAPE_0 + n, part, :] for n in range(3)]
            for y in range(Y):
                exponent = RATE * field[x, y : y + 1, :]
                for n in range(3):
                    exponent = exponent + shapes[n] * order[n, x, y : y + 1, :]
                value = jnp.exp2(exponent)
                factor[Y * x + y, part, :] = value
                cells[0, x + 1, y + 1, part, :] = value * q[Y * x + y, part, :]
        return carry

    lax.fori_loop(0, X, start, 0)

    for step in range(STEPS):
        zeros = jnp.zeros((16, LANES), F32)

        def edges(x, carry):
            out = list(carry)
            for group in range(4):
                part = pl.ds(16 * group, 16)
                for y in range(Y):
                    to = 64 * (group // 2) + 2 * (Y * x + y)
                    turned = pltpu.roll(cells[step, x + 1, y + 1, part, :], to, 1)
                    chosen = (lane == to) | (lane == lax.rem(to + 127, 128))
                    out[group % 2] = jnp.where(chosen, turned, out[group % 2])
            return tuple(out)

        first, second = lax.fori_loop(0, X, edges, (zeros, zeros))
        send_z[step, 0:16, :] = first
        send_z[step, 16:32, :] = second

        def face_y(x, carry):
            faces = jnp.concatenate([cells[step, x + 1, 1], cells[step, x + 1, Y]], axis=1)
            packed = jnp.dot(
                pack[1], jnp.concatenate(split(faces), axis=0), preferred_element_type=F32
            )
            send_y[step, 0, x] = packed[0:HALF, 0:LANES]
            send_y[step, 1, x] = packed[HALF:U, LANES : 2 * LANES]
            return carry

        lax.fori_loop(0, X, face_y, 0)
        for y in range(Y):
            faces = jnp.concatenate([cells[step, 1, y + 1], cells[step, X, y + 1]], axis=1)
            packed = jnp.dot(
                pack[0], jnp.concatenate(split(faces), axis=0), preferred_element_type=F32
            )
            send_x[step, 0, y] = packed[0:HALF, 0:LANES]
            send_x[step, 1, y] = packed[HALF:U, LANES : 2 * LANES]

        if step == 0:
            pl.semaphore_wait(barrier, 6)
        copies = []
        for n, (src, dst, axis, way) in enumerate(
            [
                (send_z.at[step], recv_z.at[step, 0], "gz", -1),
                (send_z.at[step], recv_z.at[step, 1], "gz", 1),
                (send_y.at[step, 0], recv_y.at[step, :, 0:HALF, :], "gx", -1),
                (send_y.at[step, 1], recv_y.at[step, :, HALF:U, :], "gx", 1),
                (send_x.at[step, 0], recv_x.at[step, :, 0:HALF, :], "gy", -1),
                (send_x.at[step, 1], recv_x.at[step, :, HALF:U, :], "gy", 1),
            ]
        ):
            copy = pltpu.make_async_remote_copy(
                src_ref=src, dst_ref=dst, send_sem=send_sem.at[step, n], recv_sem=recv_sem.at[step, n],
                device_id=neighbour(axis, way), device_id_type=pl.DeviceIdType.MESH,
            )
            copy.start()
            copies.append(copy)
        for copy in copies:
            copy.wait()

        def place_y(n, carry):
            received = jnp.concatenate([recv_y[step, 2 * n], recv_y[step, 2 * n + 1]], axis=1)
            chosen = jnp.dot(
                unpack[1], jnp.concatenate(split(received), axis=0), preferred_element_type=F32
            )
            for side in (0, Y + 1):
                cells[step, 2 * n + 1, side] = chosen[:, 0:LANES]
                cells[step, 2 * n + 2, side] = chosen[:, LANES : 2 * LANES]
            return carry

        lax.fori_loop(0, X // 2, place_y, 0)
        for y in range(0, Y, 2):
            received = jnp.concatenate([recv_x[step, y], recv_x[step, y + 1]], axis=1)
            chosen = jnp.dot(
                unpack[0], jnp.concatenate(split(received), axis=0), preferred_element_type=F32
            )
            for side in (0, X + 1):
                cells[step, side, y + 1] = chosen[:, 0:LANES]
                cells[step, side, y + 2] = chosen[:, LANES : 2 * LANES]

        ends = []
        for n in range(2):
            part = pl.ds(16 * n, 16)
            ends.append(
                jnp.where(
                    lax.rem(lane, 2) == 0,
                    recv_z[step, 0, part, :],
                    pltpu.roll(recv_z[step, 1, part, :], 2, 1),
                )
            )
        pltpu.make_async_copy(forward.at[step], forward.at[step], forward_sem.at[step]).wait()

        def advance(x, carry):
            parts = [([], []) for _ in range(Y)]
            for group in range(4):
                part = pl.ds(16 * group, 16)
                up_x, low_x, up_y, low_y, speed_z, kept = [coef[n, part, :] for n in range(6)]
                up_z = coef[SIGN_Z, part, :] > 0.5
                edge = ((lane == 127) & up_z) | ((lane == 0) & ~up_z)
                for y in range(Y):
                    here = cells[step, x + 1, y + 1, part, :]
                    beside = jnp.where(up_z, pltpu.roll(here, 127, 1), pltpu.roll(here, 1, 1))
                    to = lax.rem(255 - 64 * (group // 2) - 2 * (Y * x + y), 128)
                    beside = jnp.where(edge, pltpu.roll(ends[group % 2], to, 1), beside)
                    moved = (
                        kept * here
                        + up_x * cells[step, x + 2, y + 1, part, :]
                        + low_x * cells[step, x, y + 1, part, :]
                        + up_y * cells[step, x + 1, y + 2, part, :]
                        + low_y * cells[step, x + 1, y, part, :]
                        + speed_z * beside
                    )
                    high, low = split(moved)
                    parts[y][0].append(high)
                    parts[y][1].append(low)
            for y in range(0, Y, 2):
                stack = [jnp.concatenate(parts[n][0] + parts[n][1], axis=0) for n in (y, y + 1)]
                stack = jnp.concatenate(stack, axis=1)
                mixed = jnp.dot(
                    mix4[...], jnp.concatenate([stack, stack], axis=0), preferred_element_type=F32
                )
                sums = []
                for n in range(2):
                    row = Y * x + y + n
                    value = factor[row] * mixed[:, LANES * n : LANES * (n + 1)]
                    if step == 0:
                        cells[1, x + 1, y + n + 1] = factor[row] * value
                        forward[0, row] = forward[0, row] * value
                    else:
                        q[row] = value
                        total = forward[0, row] + forward[1, row] * value
                        sums.append(jnp.concatenate(split(total), axis=0))
                        pltpu.make_async_copy(
                            q.at[row], out_q.at[:, row, 0, :], store_sem.at[0]
                        ).start()
                if step == 1:
                    sums = jnp.concatenate(sums, axis=1)
                    summed = jnp.dot(
                        sum4[...], jnp.concatenate([sums, sums], axis=0), preferred_element_type=F32
                    )
                    for n in range(2):
                        for a in range(4):
                            dens[a, x, y + n : y + n + 1, :] = summed[
                                a : a + 1, LANES * n : LANES * (n + 1)
                            ]
            return carry

        lax.fori_loop(0, X, advance, 0)

    last = [
        pltpu.make_async_copy(dens.at[0], out_density, store_sem.at[1]),
        pltpu.make_async_copy(dens.at[1:4], out_order, store_sem.at[2]),
    ]
    for copy in last:
        copy.start()
    for copy in last:
        copy.wait()
    pltpu.make_async_copy(q, q, store_sem.at[0]).wait()


def body(q_dagger, forward, field_iso, field_order, sphere_step, upwind_sign, direction_size, sphere_weight):
    anywhere = pl.BlockSpec(memory_space=pl.ANY)
    cells = (U, ROWS, 1, LANES)
    q, density, order = pl.pallas_call(
        kernel,
        out_shape=(
            jax.ShapeDtypeStruct(cells, F32),
            jax.ShapeDtypeStruct(field_iso.shape, F32),
            jax.ShapeDtypeStruct(field_order.shape, F32),
        ),
        in_specs=[anywhere] * 8,
        out_specs=(anywhere,) * 3,
        scratch_shapes=[
            pltpu.VMEM((ROWS, U, LANES), F32),
            pltpu.VMEM((STEPS, ROWS, U, LANES), F32),
            pltpu.VMEM((ROWS, U, LANES), F32),
            pltpu.VMEM((X, Y, LANES), F32),
            pltpu.VMEM((3, X, Y, LANES), F32),
            pltpu.VMEM((U, U), F32),
            pltpu.VMEM((3, U), jnp.int32),
            pltpu.VMEM((3, U), F32),
            pltpu.VMEM((1, U), F32),
            pltpu.VMEM((STEPS, X + 2, Y + 2, U, LANES), F32),
            pltpu.VMEM((10, U, LANES), F32),
            pltpu.VMEM((LANES, LANES), F32),
            pltpu.VMEM((U, 4 * U), BF16),
            pltpu.VMEM((16, 4 * U), BF16),
            pltpu.VMEM((2, U, 2 * U), BF16),
            pltpu.VMEM((2, U, 2 * U), BF16),
            pltpu.VMEM((STEPS, 2, Y, HALF, LANES), F32),
            pltpu.VMEM((STEPS, 2, X, HALF, LANES), F32),
            pltpu.VMEM((STEPS, HALF, LANES), F32),
            pltpu.VMEM((STEPS, Y, U, LANES), F32),
            pltpu.VMEM((STEPS, X, U, LANES), F32),
            pltpu.VMEM((STEPS, 2, HALF, LANES), F32),
            pltpu.VMEM((4, X, Y, LANES), F32),
            pltpu.SemaphoreType.DMA((6,)),
            pltpu.SemaphoreType.DMA((1,)),
            pltpu.SemaphoreType.DMA((STEPS,)),
            pltpu.SemaphoreType.DMA((3,)),
            pltpu.SemaphoreType.DMA((STEPS, 6)),
            pltpu.SemaphoreType.DMA((STEPS, 6)),
        ],
        compiler_params=pltpu.CompilerParams(
            collective_id=0, has_side_effects=True, vmem_limit_bytes=48 * 1024 * 1024
        ),
        name="propagate",
    )(
        q_dagger.reshape(cells), forward.reshape((STEPS,) + cells), field_iso, field_order,
        sphere_step, upwind_sign, direction_size, sphere_weight.reshape(1, U),
    )
    return q.reshape(q_dagger.shape), density, order


def solution(mesh):
    grid = P("gy", "gx", "gz")
    placed = (
        P(None, "gy", "gx", "gz"), P(None, None, "gy", "gx", "gz"), grid,
        P(None, "gy", "gx", "gz"), P(), P(), P(), P(),
    )
    return jax.shard_map(
        body, mesh=mesh, in_specs=placed,
        out_specs=(P(None, "gy", "gx", "gz"), grid, P(None, "gy", "gx", "gz")), check_vma=False,
    )
```

time: 151 us -> 51.8 us (0.34)
  starting transfers between devices: 60 us -> 0 us
  Pallas kernels: 0 us -> 41.5 us
  local copies, waits for them, and re-layouts: 38 us -> 9.29 us
  waiting for transfers between devices: 23.3 us -> 0 us
  other arithmetic: 16.3 us -> 0 us
  matrix products: 11.7 us -> 0 us
    ppermute x12 -> x0, starting transfers between devices: 60 us -> none  [the longest x6 32 us: extended(): lax.ppermute(head, axis, [((i + 1) % count, i) for i in range(count)])]
    pallas_call x0 -> x1, Pallas kernels: none -> 41.5 us  [body(): pl.pallas_call(kernel, out_shape=(jax.ShapeDtypeStruct(cells, F32), jax.S...]
    ppermute x12 -> x0, waiting for transfers between devices: 23.3 us -> none  [the longest x6 16.4 us: extended(): lax.ppermute(head, axis, [((i + 1) % count, i) for i in range(count)])]
    slice x9 -> x0, local copies, waits for them, and re-layouts: 16.4 us -> none  [the longest x4 10.2 us: extended(): head = lax.slice_in_dim(cells, 0, width, axis=dim)]
    dot_general x5 -> x0, matrix products: 11.7 us -> none  [the longest x2 5.59 us: sphere_mix(): jnp.dot(sphere_step, flat, precision=lax.Precision.HIGHEST, preferred_ele...]
    ppermute x4 -> x0, local copies, waits for them, and re-layouts: 10 us -> none  [the longest x2 5.38 us: extended(): lax.ppermute(head, axis, [((i + 1) % count, i) for i in range(count)])]
    add x3 -> x0, other arithmetic: 7.05 us -> none  [the longest x2 6.43 us: advect_parts(): moved = moved + SPEED * speeds * (chosen - center)]
    reshape x4 -> x0, local copies, waits for them, and re-layouts: 6.46 us -> none  [the longest x2 3.64 us: sphere_mix(): return mixed.reshape(values.shape)]
  transfers between devices with their start and end apart: 12 -> 0, of which waited for: 10 -> 0; matrix products, arithmetic and copies ran while one was open for 7% -> 0% of each run, Pallas kernels for 0% -> 0%
where the time goes in v1:
time: 51.8 us; the launch traced here: 51.4 us
  Pallas kernels  41.5 us (80%)
  local copies, waits for them, and re-layouts  9.29 us (18%)
  between operations  0.66 us (1%)
    pallas_call x1, Pallas kernels, body(): pl.pallas_call(kernel, out_shape=(jax.ShapeDtypeStruct(cells, F32), jax.S...  41.5 us
    unnamed x19, local copies, waits for them, and re-layouts  9.29 us

profile of v1, /device:TPU:1, one launch (start us, length us, event | category | flops | bytes accessed | tf_op | source)
XLA Modules:
  0.0 51.4 jit_solution(9916163285692950506)
XLA Ops:
  0.6 0.0 copy-start
  0.6 1.6 %copy-done = f32[2,64,8,4,128]{4,3,2,1,0:T(4,128)S(1)} copy-done((f32[2,64,8,4,128]{4,3,2,1,0:T(4,128)S(1)}, f32[2,64,8,4,128]{4,3,2,1,0:T(4,128)}, u32[]{:S(2)}) %copy-start) | copy-done | bytes 2097176
  2.2 0.0 copy-start.1
  2.2 1.2 %copy-done.1 = f32[64,8,4,128]{3,2,1,0:T(4,128)S(1)} copy-done((f32[64,8,4,128]{3,2,1,0:T(4,128)S(1)}, f32[64,8,4,128]{3,2,1,0:T(4,128)}, u32[]{:S(2)}) %copy-start.1) | copy-done | bytes 1048600
  3.5 0.0 copy-start.2
  3.5 0.8 %copy-done.2 = f32[3,8,4,128]{3,2,1,0:T(4,128)S(1)} copy-done((f32[3,8,4,128]{3,2,1,0:T(4,128)S(1)}, f32[3,8,4,128]{3,2,1,0:T(4,128)}, u32[]{:S(2)}) %copy-start.2) | copy-done | bytes 49176
  4.2 0.0 copy-start.3
  4.3 0.8 %copy-done.3 = f32[64,64]{1,0:T(8,128)S(1)} copy-done((f32[64,64]{1,0:T(8,128)S(1)}, f32[64,64]{1,0:T(8,128)}, u32[]{:S(2)}) %copy-start.3) | copy-done | bytes 16408
  5.0 0.0 copy-start.4
  5.0 0.7 %copy-done.4 = f32[8,4,128]{2,1,0:T(4,128)S(1)} copy-done((f32[8,4,128]{2,1,0:T(4,128)S(1)}, f32[8,4,128]{2,1,0:T(4,128)}, u32[]{:S(2)}) %copy-start.4) | copy-done | bytes 16408
  5.7 0.0 copy-start.5
  5.7 0.7 %copy-done.5 = s32[3,64]{1,0:T(4,128)S(1)} copy-done((s32[3,64]{1,0:T(4,128)S(1)}, s32[3,64]{1,0:T(4,128)}, u32[]{:S(2)}) %copy-start.5) | copy-done | bytes 792
  6.4 0.0 copy-start.6
  6.4 0.7 %copy-done.6 = f32[3,64]{1,0:T(4,128)S(1)} copy-done((f32[3,64]{1,0:T(4,128)S(1)}, f32[3,64]{1,0:T(4,128)}, u32[]{:S(2)}) %copy-start.6) | copy-done | bytes 792
  7.1 0.0 copy-start.7
  7.1 0.7 %copy-done.7 = f32[64]{0:T(128)S(1)} copy-done((f32[64]{0:T(128)S(1)}, f32[64]{0:T(128)}, u32[]{:S(2)}) %copy-start.7) | copy-done | bytes 280
  7.7 41.5 %propagate.1 = (f32[64,32,1,128]{3,2,1,0:T(1,128)S(1)}, f32[8,4,128]{2,1,0:T(4,128)S(1)}, f32[3,8,4,128]{3,2,1,0:T(4,128)S(1)}) custom-call(f32[64,32,1,128]{3,2,1,0:T(1,128)S(1)} %bitcast.6, f32[2,64,32,1,128]{4,3,2,1,0:T(1,128)S(1)} %bitcast.4, f32[8,4,128]{2,1,0:T(4,128)S(1)} %copy-done.4, f32[3,8,4,128]{3,2,1,0:T(4,128)S(1)} %copy-done.2, ...), custom_call_target="tpu_custom_call" | custom-call | tf_op jit(solution)/shard_map/propagate/pallas_call | solution.py:309
  49.2 1.0 %copy.14 = f32[64,8,4,128]{3,2,1,0:T(4,128)} copy(f32[64,8,4,128]{3,2,1,0:T(4,128)S(1)} %bitcast.5) | data formatting | bytes 2097152
  50.2 0.6 %copy.15 = f32[8,4,128]{2,1,0:T(4,128)} copy(f32[8,4,128]{2,1,0:T(4,128)S(1)} %get-tuple-element.13) | data formatting | bytes 32768
  50.8 0.6 %copy.16 = f32[3,8,4,128]{3,2,1,0:T(4,128)} copy(f32[3,8,4,128]{3,2,1,0:T(4,128)S(1)} %get-tuple-element.14) | data formatting | bytes 98304
Async XLA Ops:
  0.6 1.6 %copy-start = (f32[2,64,8,4,128]{4,3,2,1,0:T(4,128)S(1)}, f32[2,64,8,4,128]{4,3,2,1,0:T(4,128)}, u32[]{:S(2)}) copy-start(f32[2,64,8,4,128]{4,3,2,1,0:T(4,128)} %param.9) | copy-start | bytes 6291460
  2.2 1.2 %copy-start.1 = (f32[64,8,4,128]{3,2,1,0:T(4,128)S(1)}, f32[64,8,4,128]{3,2,1,0:T(4,128)}, u32[]{:S(2)}) copy-start(f32[64,8,4,128]{3,2,1,0:T(4,128)} %param.8) | copy-start | bytes 3145732
  3.5 0.8 %copy-start.2 = (f32[3,8,4,128]{3,2,1,0:T(4,128)S(1)}, f32[3,8,4,128]{3,2,1,0:T(4,128)}, u32[]{:S(2)}) copy-start(f32[3,8,4,128]{3,2,1,0:T(4,128)} %order_hbm.1) | copy-start | bytes 147460
  4.2 0.8 %copy-start.3 = (f32[64,64]{1,0:T(8,128)S(1)}, f32[64,64]{1,0:T(8,128)}, u32[]{:S(2)}) copy-start(f32[64,64]{1,0:T(8,128)} %sphere_hbm.1) | copy-start | bytes 49156
  5.0 0.7 %copy-start.4 = (f32[8,4,128]{2,1,0:T(4,128)S(1)}, f32[8,4,128]{2,1,0:T(4,128)}, u32[]{:S(2)}) copy-start(f32[8,4,128]{2,1,0:T(4,128)} %iso_hbm.1) | copy-start | bytes 49156
  5.7 0.7 %copy-start.5 = (s32[3,64]{1,0:T(4,128)S(1)}, s32[3,64]{1,0:T(4,128)}, u32[]{:S(2)}) copy-start(s32[3,64]{1,0:T(4,128)} %sign_hbm.1) | copy-start | bytes 2308
  6.4 0.7 %copy-start.6 = (f32[3,64]{1,0:T(4,128)S(1)}, f32[3,64]{1,0:T(4,128)}, u32[]{:S(2)}) copy-start(f32[3,64]{1,0:T(4,128)} %size_hbm.1) | copy-start | bytes 2308
  7.1 0.7 %copy-start.7 = (f32[64]{0:T(128)S(1)}, f32[64]{0:T(128)}, u32[]{:S(2)}) copy-start(f32[64]{0:T(128)} %param.15) | copy-start | bytes 772

commit v2 on v1

v2 whole, which is shorter than its diff:
```python
import functools
import math

import jax
import jax.numpy as jnp
from jax import lax
from jax.experimental import pallas as pl
from jax.experimental.pallas import tpu as pltpu
from jax.sharding import PartitionSpec as P

U = 64
HALF = U // 2
LANES = 128
X = 8
Y = 4
ROWS = X * Y
STEPS = 2
RATE = -0.2 / math.log(2.0)
F32 = jnp.float32
BF16 = jnp.bfloat16

UP_X, LOW_X, UP_Y, LOW_Y, SPEED_Z, KEEP, SHAPE_0, SHAPE_1, SHAPE_2, SIGN_Z, RANK_X, RANK_Y = range(12)


def split(values):
    high = values.astype(BF16)
    low = (values - high.astype(F32)).astype(BF16)
    return high, low


def iota(shape, dim):
    return lax.broadcasted_iota(jnp.int32, shape, dim)


def neighbour(axis, step):
    count = lax.axis_size(axis)
    return {axis: lax.rem(lax.axis_index(axis) + count + step, count)}


def advance(
    step, x, cells, factor, coef, mix4, ends, forward, total, nxt=None, sum4=None, q=None, dens=None
):
    lane = iota((16, LANES), 1)
    parts = [([], []) for _ in range(Y)]
    for group in range(4):
        part = pl.ds(16 * group, 16)
        up_x, low_x, up_y, low_y, speed_z, kept = [coef[n, part, :] for n in range(6)]
        up_z = coef[SIGN_Z, part, :] > 0.5
        edge = ((lane == 127) & up_z) | ((lane == 0) & ~up_z)
        for y in range(Y):
            here = cells[x + 1, y + 1, part, :]
            beside = jnp.where(up_z, pltpu.roll(here, 127, 1), pltpu.roll(here, 1, 1))
            to = (255 - 64 * (group // 2) - 2 * (Y * x + y)) % 128
            beside = jnp.where(edge, pltpu.roll(ends[group % 2], to, 1), beside)
            moved = (
                kept * here
                + up_x * cells[x + 2, y + 1, part, :]
                + low_x * cells[x, y + 1, part, :]
                + up_y * cells[x + 1, y + 2, part, :]
                + low_y * cells[x + 1, y, part, :]
                + speed_z * beside
            )
            high, low = split(moved)
            parts[y][0].append(high)
            parts[y][1].append(low)
    for y in range(0, Y, 2):
        stack = [jnp.concatenate(parts[n][0] + parts[n][1], axis=0) for n in (y, y + 1)]
        stack = jnp.concatenate(stack, axis=1)
        mixed = jnp.dot(
            mix4[...], jnp.concatenate([stack, stack], axis=0), preferred_element_type=F32
        )
        sums = []
        for n in range(2):
            row = Y * x + y + n
            value = factor[row] * mixed[:, LANES * n : LANES * (n + 1)]
            if step == 0:
                nxt[x + 1, y + n + 1] = factor[row] * value
                total[row] = forward[row] * value
            else:
                q[row] = value
                sums.append(jnp.concatenate(split(total[row] + forward[row] * value), axis=0))
        if step == 1:
            sums = jnp.concatenate(sums, axis=1)
            summed = jnp.dot(
                sum4[...], jnp.concatenate([sums, sums], axis=0), preferred_element_type=F32
            )
            for n in range(2):
                for a in range(4):
                    dens[a, x, y + n : y + n + 1, :] = summed[
                        a : a + 1, LANES * n : LANES * (n + 1)
                    ]


def z_ends(recv, slot=None):
    lane = iota((16, LANES), 1)
    ends = []
    for n in range(2):
        part = pl.ds(16 * n, 16)
        ends.append(
            jnp.where(
                lax.rem(lane, 2) == 0, recv[0, part, :], pltpu.roll(recv[1, part, :], 2, 1)
            )
        )
    return ends


def finish(
    cells, factor, total, forward, coef, mix4, sum4, ends,
    out_q, out_density, out_order, q, dens, store_sem,
):
    copies = []
    edge = [ends[0:16, :], ends[16:32, :]]
    for x in range(X):
        advance(1, x, cells, factor, coef, mix4, edge, forward, total, sum4=sum4, q=q, dens=dens)
        for row in range(Y * x, Y * x + Y):
            copy = pltpu.make_async_copy(q.at[row], out_q.at[:, row, 0, :], store_sem.at[row])
            copy.start()
            copies.append(copy)
    for copy in (
        pltpu.make_async_copy(dens.at[0], out_density, store_sem.at[ROWS]),
        pltpu.make_async_copy(dens.at[1:4], out_order, store_sem.at[ROWS + 1]),
    ):
        copy.start()
        copies.append(copy)
    for copy in copies:
        copy.wait()


def kernel(
    q_hbm, forward_hbm, iso_hbm, order_hbm, sphere_hbm, sign_hbm, size_hbm, weight_hbm,
    nxt, factor, total, forward_1, coef, mix4, sum4, ends_out,
    q, forward_0, field, order, sphere, sign, size, weight,
    first, table, pack, unpack,
    send_x, send_y, send_z, recv_x, recv_y, recv_z,
    load_sem, q_sem, forward_sem, send_sem, recv_sem,
):
    forward = (forward_0, forward_1)
    grids = (first, nxt)
    sides = [("gx", 1), ("gx", -1), ("gy", 1), ("gy", -1), ("gz", 1), ("gz", -1)]
    barrier = pltpu.get_barrier_semaphore()
    for axis, step in sides:
        pl.semaphore_signal(
            barrier, inc=1, device_id=neighbour(axis, step), device_id_type=pl.DeviceIdType.MESH
        )

    small = [
        pltpu.make_async_copy(src, dst, load_sem.at[n])
        for n, (src, dst) in enumerate(
            [(sign_hbm, sign), (size_hbm, size), (weight_hbm, weight), (sphere_hbm, sphere),
             (iso_hbm, field), (order_hbm, order)]
        )
    ]
    for copy in small:
        copy.start()

    def load_q(row, carry):
        pltpu.make_async_copy(q_hbm.at[:, row, 0, :], q.at[row], q_sem.at[0]).start()
        return carry

    lax.fori_loop(0, ROWS, load_q, 0)

    def load_forward(row, carry):
        for step in range(STEPS):
            pltpu.make_async_copy(
                forward_hbm.at[step, :, row, 0, :], forward[step].at[row], forward_sem.at[step]
            ).start()
        return carry

    lax.fori_loop(0, ROWS, load_forward, 0)

    for copy in small:
        copy.wait()
    signs = sign[...].astype(F32)
    signed = (2.0 * signs - 1.0) * size[...]
    length = jnp.sqrt(jnp.sum(signed * signed, axis=0, keepdims=True))
    along = signed / length
    shape = along * along - 1.0 / 3.0
    speed = 0.5 * jnp.abs(along)
    below = (iota((U, U), 0) < iota((U, U), 1)).astype(BF16)
    ones_before = jnp.dot(signs.astype(BF16), below, preferred_element_type=F32)
    place = iota((1, U), 1).astype(F32)
    rank = jnp.where(signs > 0.5, ones_before, HALF + place - ones_before)
    keep = 1.0 - jnp.sum(speed, axis=0, keepdims=True)
    upper = speed * signs
    lower = speed * (1.0 - signs)
    rows = [
        upper[0:1], lower[0:1], upper[1:2], lower[1:2], speed[2:3], keep,
        RATE * shape[0:1], RATE * shape[1:2], RATE * shape[2:3],
        signs[2:3], rank[0:1], rank[1:2],
    ]
    stacked = jnp.zeros((16, U), F32)
    which = iota((16, U), 0)
    for n, row in enumerate(rows):
        stacked = jnp.where(which == n, row, stacked)
    table[...] = jnp.zeros((LANES, LANES), F32)
    table[0:16, 0:U] = stacked
    columns = jnp.transpose(table[...])
    for n in range(10):
        coef[n] = jnp.broadcast_to(columns[0:U, n : n + 1], (U, LANES))
    half_weight = weight[...] / STEPS
    sums = jnp.zeros((16, U), F32)
    for n, row in enumerate(
        [half_weight, half_weight * shape[0:1], half_weight * shape[1:2], half_weight * shape[2:3]]
    ):
        sums = jnp.where(which == n, row, sums)
    high, low = split(sums)
    sum4[...] = jnp.concatenate([high, high, low, low], axis=1)
    high, low = split(sphere[...])
    mix4[...] = jnp.concatenate([high, high, low, low], axis=1)
    for axis in range(2):
        to_rank = (iota((U, U), 0).astype(F32) == rank[axis : axis + 1]).astype(BF16)
        pack[axis] = jnp.concatenate([to_rank, to_rank], axis=1)
        from_rank = (
            iota((U, LANES), 1).astype(F32) == columns[0:U, RANK_X + axis : RANK_X + axis + 1]
        ) | (
            (iota((U, LANES), 1) - U).astype(F32) == columns[0:U, RANK_X + axis : RANK_X + axis + 1]
        )
        unpack[axis] = from_rank.astype(BF16)

    lane = iota((16, LANES), 1)

    pltpu.make_async_copy(q, q, q_sem.at[0]).wait()

    def start(x, carry):
        for group in range(4):
            part = pl.ds(16 * group, 16)
            shapes = [coef[SHAPE_0 + n, part, :] for n in range(3)]
            for y in range(Y):
                exponent = RATE * field[x, y : y + 1, :]
                for n in range(3):
                    exponent = exponent + shapes[n] * order[n, x, y : y + 1, :]
                value = jnp.exp2(exponent)
                factor[Y * x + y, part, :] = value
                first[x + 1, y + 1, part, :] = value * q[Y * x + y, part, :]
        return carry

    lax.fori_loop(0, X, start, 0, unroll=True)

    waits = []
    for step in range(STEPS):
        cells = grids[step]
        zeros = jnp.zeros((16, LANES), F32)

        def edges(x, carry):
            out = list(carry)
            for group in range(4):
                part = pl.ds(16 * group, 16)
                for y in range(Y):
                    to = 64 * (group // 2) + 2 * (Y * x + y)
                    turned = pltpu.roll(cells[x + 1, y + 1, part, :], to, 1)
                    chosen = (lane == to) | (lane == lax.rem(to + 127, 128))
                    out[group % 2] = jnp.where(chosen, turned, out[group % 2])
            return tuple(out)

        top, bottom = lax.fori_loop(0, X, edges, (zeros, zeros), unroll=True)
        send_z[step, 0:16, :] = top
        send_z[step, 16:32, :] = bottom

        def face_y(x, carry):
            faces = jnp.concatenate([cells[x + 1, 1], cells[x + 1, Y]], axis=1)
            packed = jnp.dot(
                pack[1], jnp.concatenate(split(faces), axis=0), preferred_element_type=F32
            )
            send_y[step, 0, x] = packed[0:HALF, 0:LANES]
            send_y[step, 1, x] = packed[HALF:U, LANES : 2 * LANES]
            return carry

        lax.fori_loop(0, X, face_y, 0, unroll=True)
        for y in range(Y):
            faces = jnp.concatenate([cells[1, y + 1], cells[X, y + 1]], axis=1)
            packed = jnp.dot(
                pack[0], jnp.concatenate(split(faces), axis=0), preferred_element_type=F32
            )
            send_x[step, 0, y] = packed[0:HALF, 0:LANES]
            send_x[step, 1, y] = packed[HALF:U, LANES : 2 * LANES]

        if step == 0:
            pl.semaphore_wait(barrier, 6)
        copies = []
        for n, (src, dst, axis, way) in enumerate(
            [
                (send_z.at[step], recv_z.at[step, 0], "gz", -1),
                (send_z.at[step], recv_z.at[step, 1], "gz", 1),
                (send_y.at[step, 0], recv_y.at[step, :, 0:HALF, :], "gx", -1),
                (send_y.at[step, 1], recv_y.at[step, :, HALF:U, :], "gx", 1),
                (send_x.at[step, 0], recv_x.at[step, :, 0:HALF, :], "gy", -1),
                (send_x.at[step, 1], recv_x.at[step, :, HALF:U, :], "gy", 1),
            ]
        ):
            copy = pltpu.make_async_remote_copy(
                src_ref=src, dst_ref=dst, send_sem=send_sem.at[step, n], recv_sem=recv_sem.at[step, n],
                device_id=neighbour(axis, way), device_id_type=pl.DeviceIdType.MESH,
            )
            copy.start()
            copies.append(copy)
        for copy in copies:
            copy.wait_recv()
        waits += copies

        def place_y(n, carry):
            received = jnp.concatenate([recv_y[step, 2 * n], recv_y[step, 2 * n + 1]], axis=1)
            chosen = jnp.dot(
                unpack[1], jnp.concatenate(split(received), axis=0), preferred_element_type=F32
            )
            for side in (0, Y + 1):
                cells[2 * n + 1, side] = chosen[:, 0:LANES]
                cells[2 * n + 2, side] = chosen[:, LANES : 2 * LANES]
            return carry

        lax.fori_loop(0, X // 2, place_y, 0, unroll=True)
        for y in range(0, Y, 2):
            received = jnp.concatenate([recv_x[step, y], recv_x[step, y + 1]], axis=1)
            chosen = jnp.dot(
                unpack[0], jnp.concatenate(split(received), axis=0), preferred_element_type=F32
            )
            for side in (0, X + 1):
                cells[side, y + 1] = chosen[:, 0:LANES]
                cells[side, y + 2] = chosen[:, LANES : 2 * LANES]

        ends = z_ends(recv_z.at[step])
        pltpu.make_async_copy(forward[step], forward[step], forward_sem.at[step]).wait()
        if step == 0:
            for x in range(X):
                advance(0, x, first, factor, coef, mix4, ends, forward_0, total, nxt=nxt)
        else:
            ends_out[0:16, :] = ends[0]
            ends_out[16:32, :] = ends[1]
    for copy in waits:
        copy.wait_send()


def body(q_dagger, forward, field_iso, field_order, sphere_step, upwind_sign, direction_size, sphere_weight):
    anywhere = pl.BlockSpec(memory_space=pl.ANY)
    inside = pl.BlockSpec(memory_space=pltpu.VMEM)
    cells = (U, ROWS, 1, LANES)
    outer = [
        ((X + 2, Y + 2, U, LANES), F32), ((ROWS, U, LANES), F32), ((ROWS, U, LANES), F32),
        ((ROWS, U, LANES), F32), ((10, U, LANES), F32), ((U, 4 * U), BF16), ((16, 4 * U), BF16),
        ((HALF, LANES), F32),
    ]
    held = pl.pallas_call(
        kernel,
        out_shape=tuple(pltpu.VMEM(shape, kind) for shape, kind in outer),
        in_specs=[pl.BlockSpec(memory_space=pltpu.HBM)] * 8,
        out_specs=(inside,) * 8,
        scratch_shapes=[
            pltpu.VMEM((ROWS, U, LANES), F32),
            pltpu.VMEM((ROWS, U, LANES), F32),
            pltpu.VMEM((X, Y, LANES), F32),
            pltpu.VMEM((3, X, Y, LANES), F32),
            pltpu.VMEM((U, U), F32),
            pltpu.VMEM((3, U), jnp.int32),
            pltpu.VMEM((3, U), F32),
            pltpu.VMEM((1, U), F32),
            pltpu.VMEM((X + 2, Y + 2, U, LANES), F32),
            pltpu.VMEM((LANES, LANES), F32),
            pltpu.VMEM((2, U, 2 * U), BF16),
            pltpu.VMEM((2, U, 2 * U), BF16),
            pltpu.VMEM((STEPS, 2, Y, HALF, LANES), F32),
            pltpu.VMEM((STEPS, 2, X, HALF, LANES), F32),
            pltpu.VMEM((STEPS, HALF, LANES), F32),
            pltpu.VMEM((STEPS, Y, U, LANES), F32),
            pltpu.VMEM((STEPS, X, U, LANES), F32),
            pltpu.VMEM((STEPS, 2, HALF, LANES), F32),
            pltpu.SemaphoreType.DMA((6,)),
            pltpu.SemaphoreType.DMA((1,)),
            pltpu.SemaphoreType.DMA((STEPS,)),
            pltpu.SemaphoreType.DMA((STEPS, 6)),
            pltpu.SemaphoreType.DMA((STEPS, 6)),
        ],
        compiler_params=pltpu.CompilerParams(
            collective_id=0, has_side_effects=True, vmem_limit_bytes=32 * 1024 * 1024
        ),
        name="propagate",
    )(
        *[pltpu.with_memory_space_constraint(array, pltpu.HBM) for array in (
            q_dagger.reshape(cells), forward.reshape((STEPS,) + cells), field_iso, field_order,
            sphere_step, upwind_sign, direction_size, sphere_weight.reshape(1, U),
        )]
    )
    q, density, order = pl.pallas_call(
        finish,
        out_shape=(
            jax.ShapeDtypeStruct(cells, F32),
            jax.ShapeDtypeStruct(field_iso.shape, F32),
            jax.ShapeDtypeStruct(field_order.shape, F32),
        ),
        in_specs=[inside] * 8,
        out_specs=(pl.BlockSpec(memory_space=pltpu.HBM),) * 3,
        scratch_shapes=[
            pltpu.VMEM((ROWS, U, LANES), F32),
            pltpu.VMEM((4, X, Y, LANES), F32),
            pltpu.SemaphoreType.DMA((ROWS + 2,)),
        ],
        compiler_params=pltpu.CompilerParams(vmem_limit_bytes=32 * 1024 * 1024),
        name="finish",
    )(*held)
    return q.reshape(q_dagger.shape), density, order


def solution(mesh):
    grid = P("gy", "gx", "gz")
    placed = (
        P(None, "gy", "gx", "gz"), P(None, None, "gy", "gx", "gz"), grid,
        P(None, "gy", "gx", "gz"), P(), P(), P(), P(),
    )
    return jax.shard_map(
        body, mesh=mesh, in_specs=placed,
        out_specs=(P(None, "gy", "gx", "gz"), grid, P(None, "gy", "gx", "gz")), check_vma=False,
    )
```

time: 51.8 us -> 31.4 us (0.61)
  Pallas kernels: 41.5 us -> 30.6 us
  local copies, waits for them, and re-layouts: 9.29 us -> 0 us
    pallas_call x1 -> x2, Pallas kernels: 41.5 us -> 30.6 us  [the longest x1 28.3 us: body(): pl.pallas_call(kernel, out_shape=tuple((pltpu.VMEM(shape, kind) for shape...]
    unnamed x19 -> x0, local copies, waits for them, and re-layouts: 9.29 us -> none
where the time goes in v2:
time: 31.4 us; the launch traced here: 31.2 us
  Pallas kernels  30.6 us (97%)
  between operations  0.64 us (2%)
    pallas_call x1, Pallas kernels, body(): pl.pallas_call(kernel, out_shape=tuple((pltpu.VMEM(shape, kind) for shape...  28.3 us
    pallas_call x1, Pallas kernels, body(): pl.pallas_call(finish, out_shape=(jax.ShapeDtypeStruct(cells, F32), jax.S...  2.3 us

profile of v2, /device:TPU:1, one launch (start us, length us, event | category | flops | bytes accessed | tf_op | source)
XLA Modules:
  0.0 31.2 jit_solution(897753422188563067)
XLA Ops:
  0.6 28.3 %propagate.1 = (f32[10,6,64,128]{3,2,1,0:T(8,128)S(1)}, f32[32,64,128]{2,1,0:T(8,128)S(1)}, f32[32,64,128]{2,1,0:T(8,128)S(1)}, f32[32,64,128]{2,1,0:T(8,128)S(1...) custom-call(f32[64,32,1,128]{3,2,1,0:T(1,128)} %bitcast.5, ...), custom_call_target="tpu_custom_call" | custom-call | tf_op jit(solution)/shard_map/propagate/pallas_call | solution.py:341
  28.9 2.3 %finish.1 = (f32[64,32,1,128]{3,2,1,0:T(1,128)}, f32[8,4,128]{2,1,0:T(4,128)}, f32[3,8,4,128]{3,2,1,0:T(4,128)}) custom-call(f32[10,6,64,128]{3,2,1,0:T(8,128)S(1)} %get-tuple-element.14.cells, f32[32,64,128]{2,1,0:T(8,128)S(1)} %get-tuple-element.15.factor, f32[32,64,128]{2,1,0:T(8,128)S(1)} %get-tuple-element.16.total, ...), custom_call_target="tpu_custom_call" | custom-call | tf_op jit(solution)/shard_map/finish/pallas_call | solution.py:381

commit v3 on v2

v3 whole, which is shorter than its diff:
```python
import functools
import math

import jax
import jax.numpy as jnp
from jax import lax
from jax.experimental import pallas as pl
from jax.experimental.pallas import tpu as pltpu
from jax.sharding import PartitionSpec as P

U = 64
HALF = U // 2
LANES = 128
X = 8
Y = 4
ROWS = X * Y
STEPS = 2
RATE = -0.2 / math.log(2.0)
F32 = jnp.float32
BF16 = jnp.bfloat16

UP_X, LOW_X, UP_Y, LOW_Y, SPEED_Z, KEEP, SHAPE_0, SHAPE_1, SHAPE_2, SIGN_Z, RANK_X, RANK_Y = range(12)


def split(values):
    high = values.astype(BF16)
    low = (values - high.astype(F32)).astype(BF16)
    return high, low


def iota(shape, dim):
    return lax.broadcasted_iota(jnp.int32, shape, dim)


def neighbour(axis, step):
    count = lax.axis_size(axis)
    return {axis: lax.rem(lax.axis_index(axis) + count + step, count)}


def stacked4(values):
    pair = jnp.concatenate(split(values), axis=0)
    return jnp.concatenate([pair, pair], axis=0)


def mix_own(x, cells, coef, mix4, mixed):
    lane = iota((16, LANES), 1)
    parts = [([], []) for _ in range(Y)]
    for group in range(4):
        part = pl.ds(16 * group, 16)
        up_x, low_x, up_y, low_y, speed_z, kept = [coef[n, part, :] for n in range(6)]
        up_z = coef[SIGN_Z, part, :] > 0.5
        up_speed = jnp.where(up_z & (lane != 127), speed_z, 0.0)
        low_speed = jnp.where(~up_z & (lane != 0), speed_z, 0.0)
        for y in range(Y):
            here = cells[x, y, part, :]
            moved = (
                kept * here
                + up_speed * pltpu.roll(here, 127, 1)
                + low_speed * pltpu.roll(here, 1, 1)
            )
            if x + 1 < X:
                moved = moved + up_x * cells[x + 1, y, part, :]
            if x > 0:
                moved = moved + low_x * cells[x - 1, y, part, :]
            if y + 1 < Y:
                moved = moved + up_y * cells[x, y + 1, part, :]
            if y > 0:
                moved = moved + low_y * cells[x, y - 1, part, :]
            high, low = split(moved)
            parts[y][0].append(high)
            parts[y][1].append(low)
    for y in range(0, Y, 2):
        stack = [jnp.concatenate(parts[n][0] + parts[n][1], axis=0) for n in (y, y + 1)]
        stack = jnp.concatenate(stack, axis=1)
        out = jnp.dot(
            mix4[...], jnp.concatenate([stack, stack], axis=0), preferred_element_type=F32
        )
        for n in range(2):
            mixed[Y * x + y + n] = out[:, LANES * n : LANES * (n + 1)]


def mix_ends(recv, coef, mix4):
    lane = iota((HALF, LANES), 1)
    ends = jnp.where(lane % 2 == 0, recv[0], pltpu.roll(recv[1], 2, 1))
    ends = jnp.concatenate([ends, pltpu.roll(ends, 64, 1)], axis=0)
    upper = iota((U, LANES), 1) % 2 == 0
    wanted = upper == (coef[SIGN_Z] > 0.5)
    ends = jnp.where(wanted, coef[SPEED_Z] * ends, 0.0)
    return jnp.dot(mix4[...], stacked4(ends), preferred_element_type=F32)


def add_sides(recv, side4, mixed, rows):
    for way in range(2):
        part = pl.ds(HALF * way, HALF)
        for place in range(0, len(rows[way]), 2):
            pair = jnp.concatenate([recv[place, part, :], recv[place + 1, part, :]], axis=1)
            out = jnp.dot(side4[way], stacked4(pair), preferred_element_type=F32)
            for n in range(2):
                row = rows[way][place + n]
                mixed[row] = mixed[row] + out[:, LANES * n : LANES * (n + 1)]


def whole(row, mixed, end_terms):
    lane = iota((U, LANES), 1)
    edge = (lane == 0) | (lane == 127)
    return mixed[row] + jnp.where(edge, pltpu.roll(end_terms, (127 - 2 * row) % 128, 1), 0.0)


def finish(
    mixed, factor, total, forward, sum4, end_terms, out_q, out_density, out_order, q, dens, store_sem
):
    copies = []
    terms = end_terms[...]
    for first in range(0, ROWS, 2):
        sums = []
        for row in (first, first + 1):
            value = factor[row] * whole(row, mixed, terms)
            q[row] = value
            copy = pltpu.make_async_copy(q.at[row], out_q.at[:, row, 0, :], store_sem.at[row])
            copy.start()
            copies.append(copy)
            sums.append(jnp.concatenate(split(total[row] + forward[row] * value), axis=0))
        sums = jnp.concatenate(sums, axis=1)
        summed = jnp.dot(
            sum4[...], jnp.concatenate([sums, sums], axis=0), preferred_element_type=F32
        )
        for n in range(2):
            x, y = divmod(first + n, Y)
            for a in range(4):
                dens[a, x, y : y + 1, :] = summed[a : a + 1, LANES * n : LANES * (n + 1)]
    for copy in (
        pltpu.make_async_copy(dens.at[0], out_density, store_sem.at[ROWS]),
        pltpu.make_async_copy(dens.at[1:4], out_order, store_sem.at[ROWS + 1]),
    ):
        copy.start()
        copies.append(copy)
    for copy in copies:
        copy.wait()


def kernel(
    q_hbm, forward_hbm, iso_hbm, order_hbm, sphere_hbm, sign_hbm, size_hbm, weight_hbm,
    mixed, factor, total, forward_1, sum4, terms_out,
    q, forward_0, field, order, sphere, sign, size, weight,
    cells_0, cells_1, coef, table, mix4, pack, side4,
    send_x, send_y, send_z, recv_x, recv_y, recv_z,
    load_sem, q_sem, forward_sem, send_sem, recv_sem,
):
    forward = (forward_0, forward_1)
    grids = (cells_0, cells_1)
    barrier = pltpu.get_barrier_semaphore()
    for axis in ("gx", "gy", "gz"):
        for way in (1, -1):
            pl.semaphore_signal(
                barrier, inc=1, device_id=neighbour(axis, way), device_id_type=pl.DeviceIdType.MESH
            )

    small = [
        pltpu.make_async_copy(src, dst, load_sem.at[n])
        for n, (src, dst) in enumerate(
            [(sign_hbm, sign), (size_hbm, size), (iso_hbm, field), (order_hbm, order),
             (weight_hbm, weight), (sphere_hbm, sphere)]
        )
    ]
    for copy in small:
        copy.start()

    def load_q(row, carry):
        pltpu.make_async_copy(q_hbm.at[:, row, 0, :], q.at[row], q_sem.at[0]).start()
        return carry

    lax.fori_loop(0, ROWS, load_q, 0)

    small[0].wait()
    small[1].wait()
    signs = sign[...].astype(F32)
    signed = (2.0 * signs - 1.0) * size[...]
    length = jnp.sqrt(jnp.sum(signed * signed, axis=0, keepdims=True))
    along = signed / length
    shape = along * along - 1.0 / 3.0
    speed = 0.5 * jnp.abs(along)
    below = (iota((U, U), 0) < iota((U, U), 1)).astype(BF16)
    ones_before = jnp.dot(signs.astype(BF16), below, preferred_element_type=F32)
    place = iota((1, U), 1).astype(F32)
    rank = jnp.where(signs > 0.5, ones_before, HALF + place - ones_before)
    keep = 1.0 - jnp.sum(speed, axis=0, keepdims=True)
    upper = speed * signs
    lower = speed * (1.0 - signs)
    rows = [
        upper[0:1], lower[0:1], upper[1:2], lower[1:2], speed[2:3], keep,
        RATE * shape[0:1], RATE * shape[1:2], RATE * shape[2:3],
        signs[2:3], rank[0:1], rank[1:2],
    ]
    stacked = jnp.zeros((16, U), F32)
    which = iota((16, U), 0)
    for n, row in enumerate(rows):
        stacked = jnp.where(which == n, row, stacked)
    table[...] = jnp.zeros((LANES, LANES), F32)
    table[0:16, 0:U] = stacked
    columns = jnp.transpose(table[...])
    for n in range(10):
        coef[n] = jnp.broadcast_to(columns[0:U, n : n + 1], (U, LANES))
    for axis in range(2):
        to_rank = (iota((U, U), 0).astype(F32) == rank[axis : axis + 1]).astype(BF16)
        pack[axis] = jnp.concatenate([to_rank, to_rank], axis=1)

    lane = iota((16, LANES), 1)

    small[2].wait()
    small[3].wait()
    pltpu.make_async_copy(q, q, q_sem.at[0]).wait()
    for x in range(X):
        for group in range(4):
            part = pl.ds(16 * group, 16)
            shapes = [coef[SHAPE_0 + n, part, :] for n in range(3)]
            for y in range(Y):
                exponent = RATE * field[x, y : y + 1, :]
                for n in range(3):
                    exponent = exponent + shapes[n] * order[n, x, y : y + 1, :]
                value = jnp.exp2(exponent)
                factor[Y * x + y, part, :] = value
                cells_0[x, y, part, :] = value * q[Y * x + y, part, :]

    waits = []
    for step in range(STEPS):
        cells = grids[step]

        def send(n, src, dst, axis, way):
            copy = pltpu.make_async_remote_copy(
                src_ref=src, dst_ref=dst, send_sem=send_sem.at[step, n], recv_sem=recv_sem.at[step, n],
                device_id=neighbour(axis, way), device_id_type=pl.DeviceIdType.MESH,
            )
            copy.start()
            waits.append(copy)
            return copy

        ends = [jnp.zeros((16, LANES), F32)] * 2
        for x in range(X):
            for group in range(4):
                part = pl.ds(16 * group, 16)
                for y in range(Y):
                    to = 64 * (group // 2) + 2 * (Y * x + y)
                    turned = pltpu.roll(cells[x, y, part, :], to, 1)
                    chosen = (lane == to) | (lane == (to + 127) % 128)
                    ends[group % 2] = jnp.where(chosen, turned, ends[group % 2])
        send_z[step, 0:16, :] = ends[0]
        send_z[step, 16:32, :] = ends[1]
        if step == 0:
            pl.semaphore_wait(barrier, 6)
        come_z = [
            send(0, send_z.at[step], recv_z.at[step, 0], "gz", -1),
            send(1, send_z.at[step], recv_z.at[step, 1], "gz", 1),
        ]
        for x in range(X):
            faces = jnp.concatenate([cells[x, 0], cells[x, Y - 1]], axis=1)
            packed = jnp.dot(
                pack[1], jnp.concatenate(split(faces), axis=0), preferred_element_type=F32
            )
            send_y[step, 0, x] = packed[0:HALF, 0:LANES]
            send_y[step, 1, x] = packed[HALF:U, LANES : 2 * LANES]
        come_y = [
            send(2, send_y.at[step, 0], recv_y.at[step, :, 0:HALF, :], "gx", -1),
            send(3, send_y.at[step, 1], recv_y.at[step, :, HALF:U, :], "gx", 1),
        ]
        for y in range(Y):
            faces = jnp.concatenate([cells[0, y], cells[X - 1, y]], axis=1)
            packed = jnp.dot(
                pack[0], jnp.concatenate(split(faces), axis=0), preferred_element_type=F32
            )
            send_x[step, 0, y] = packed[0:HALF, 0:LANES]
            send_x[step, 1, y] = packed[HALF:U, LANES : 2 * LANES]
        come_x = [
            send(4, send_x.at[step, 0], recv_x.at[step, :, 0:HALF, :], "gy", -1),
            send(5, send_x.at[step, 1], recv_x.at[step, :, HALF:U, :], "gy", 1),
        ]

        if step == 0:
            def load_forward(row, carry):
                for n in range(STEPS):
                    pltpu.make_async_copy(
                        forward_hbm.at[n, :, row, 0, :], forward[n].at[row], forward_sem.at[n]
                    ).start()
                return carry

            lax.fori_loop(0, ROWS, load_forward, 0)
            small[4].wait()
            small[5].wait()
            half_weight = weight[...] / STEPS
            sums = jnp.zeros((16, U), F32)
            for n, row in enumerate(
                [half_weight] + [half_weight * shape[a : a + 1] for a in range(3)]
            ):
                sums = jnp.where(which == n, row, sums)
            high, low = split(sums)
            sum4[...] = jnp.concatenate([high, high, low, low], axis=1)
            high, low = split(sphere[...])
            mix4[...] = jnp.concatenate([high, high, low, low], axis=1)
            for axis in range(2):
                of_rank = columns[0:U, RANK_X + axis : RANK_X + axis + 1]
                from_rank = (iota((U, U), 1).astype(F32) == of_rank).astype(BF16)
                high, low = split(sphere[...] * speed[axis : axis + 1])
                sorted_mix = jnp.dot(
                    jnp.concatenate([high, low], axis=1),
                    jnp.concatenate([from_rank, from_rank], axis=0),
                    preferred_element_type=F32,
                )
                for way in range(2):
                    high, low = split(sorted_mix[:, HALF * way : HALF * (way + 1)])
                    side4[axis, way] = jnp.concatenate([high, high, low, low], axis=1)

        for x in range(X):
            mix_own(x, cells, coef, mix4, mixed)
        if step == 0:
            for n in range(STEPS):
                pltpu.make_async_copy(forward[n], forward[n], forward_sem.at[n]).wait()

        for copy in come_z:
            copy.wait_recv()
        terms = mix_ends(recv_z.at[step], coef, mix4)
        for copy in come_x:
            copy.wait_recv()
        add_sides(
            recv_x.at[step], side4.at[0], mixed,
            [[Y * (X - 1) + y for y in range(Y)], list(range(Y))],
        )
        for copy in come_y:
            copy.wait_recv()
        add_sides(
            recv_y.at[step], side4.at[1], mixed,
            [[Y * x + Y - 1 for x in range(X)], [Y * x for x in range(X)]],
        )
        if step == 0:
            for row in range(ROWS):
                value = factor[row] * whole(row, mixed, terms)
                cells_1[row // Y, row % Y] = factor[row] * value
                total[row] = forward_0[row] * value
        else:
            terms_out[...] = terms
    for copy in waits:
        copy.wait_send()


def body(q_dagger, forward, field_iso, field_order, sphere_step, upwind_sign, direction_size, sphere_weight):
    outside = pl.BlockSpec(memory_space=pltpu.HBM)
    inside = pl.BlockSpec(memory_space=pltpu.VMEM)
    cells = (U, ROWS, 1, LANES)
    block = pltpu.VMEM((ROWS, U, LANES), F32)
    held = pl.pallas_call(
        kernel,
        out_shape=(
            block, block, block, block, pltpu.VMEM((16, 4 * U), BF16), pltpu.VMEM((U, LANES), F32)
        ),
        in_specs=[outside] * 8,
        out_specs=(inside,) * 6,
        scratch_shapes=[
            block,
            block,
            pltpu.VMEM((X, Y, LANES), F32),
            pltpu.VMEM((3, X, Y, LANES), F32),
            pltpu.VMEM((U, U), F32),
            pltpu.VMEM((3, U), jnp.int32),
            pltpu.VMEM((3, U), F32),
            pltpu.VMEM((1, U), F32),
            pltpu.VMEM((X, Y, U, LANES), F32),
            pltpu.VMEM((X, Y, U, LANES), F32),
            pltpu.VMEM((10, U, LANES), F32),
            pltpu.VMEM((LANES, LANES), F32),
            pltpu.VMEM((U, 4 * U), BF16),
            pltpu.VMEM((2, U, 2 * U), BF16),
            pltpu.VMEM((2, 2, U, LANES), BF16),
            pltpu.VMEM((STEPS, 2, Y, HALF, LANES), F32),
            pltpu.VMEM((STEPS, 2, X, HALF, LANES), F32),
            pltpu.VMEM((STEPS, HALF, LANES), F32),
            pltpu.VMEM((STEPS, Y, U, LANES), F32),
            pltpu.VMEM((STEPS, X, U, LANES), F32),
            pltpu.VMEM((STEPS, 2, HALF, LANES), F32),
            pltpu.SemaphoreType.DMA((6,)),
            pltpu.SemaphoreType.DMA((1,)),
            pltpu.SemaphoreType.DMA((STEPS,)),
            pltpu.SemaphoreType.DMA((STEPS, 6)),
            pltpu.SemaphoreType.DMA((STEPS, 6)),
        ],
        compiler_params=pltpu.CompilerParams(
            collective_id=0, has_side_effects=True, vmem_limit_bytes=32 * 1024 * 1024
        ),
        name="propagate",
    )(
        *[pltpu.with_memory_space_constraint(array, pltpu.HBM) for array in (
            q_dagger.reshape(cells), forward.reshape((STEPS,) + cells), field_iso, field_order,
            sphere_step, upwind_sign, direction_size, sphere_weight.reshape(1, U),
        )]
    )
    q, density, order = pl.pallas_call(
        finish,
        out_shape=(
            jax.ShapeDtypeStruct(cells, F32),
            jax.ShapeDtypeStruct(field_iso.shape, F32),
            jax.ShapeDtypeStruct(field_order.shape, F32),
        ),
        in_specs=[inside] * 6,
        out_specs=(outside,) * 3,
        scratch_shapes=[
            block,
            pltpu.VMEM((4, X, Y, LANES), F32),
            pltpu.SemaphoreType.DMA((ROWS + 2,)),
        ],
        compiler_params=pltpu.CompilerParams(vmem_limit_bytes=32 * 1024 * 1024),
        name="finish",
    )(*held)
    return q.reshape(q_dagger.shape), density, order


def solution(mesh):
    grid = P("gy", "gx", "gz")
    placed = (
        P(None, "gy", "gx", "gz"), P(None, None, "gy", "gx", "gz"), grid,
        P(None, "gy", "gx", "gz"), P(), P(), P(), P(),
    )
    return jax.shard_map(
        body, mesh=mesh, in_specs=placed,
        out_specs=(P(None, "gy", "gx", "gz"), grid, P(None, "gy", "gx", "gz")), check_vma=False,
    )
```

time: 31.4 us -> 30.4 us (0.968)
  Pallas kernels: 30.6 us -> 29.4 us
    pallas_call x1, Pallas kernels: 2.3 us -> 1.46 us  [body(): pl.pallas_call(finish, out_shape=(jax.ShapeDtypeStruct(cells, F32), jax.S...]
    pallas_call x1, Pallas kernels: 28.3 us -> 28 us  [body(): pl.pallas_call(kernel, out_shape=(block, block, block, block, pltpu.VMEM(...]
where the time goes in v3:
time: 30.4 us; the launch traced here: 30.1 us
  Pallas kernels  29.4 us (97%)
  between operations  0.64 us (2%)
    pallas_call x1, Pallas kernels, body(): pl.pallas_call(kernel, out_shape=(block, block, block, block, pltpu.VMEM(...  28 us
    pallas_call x1, Pallas kernels, body(): pl.pallas_call(finish, out_shape=(jax.ShapeDtypeStruct(cells, F32), jax.S...  1.46 us

profile of v3, /device:TPU:1, one launch (start us, length us, event | category | flops | bytes accessed | tf_op | source)
XLA Modules:
  0.0 30.1 jit_solution(714592224138756829)
XLA Ops:
  0.6 28.0 %propagate.1 = (f32[32,64,128]{2,1,0:T(8,128)S(1)}, f32[32,64,128]{2,1,0:T(8,128)S(1)}, f32[32,64,128]{2,1,0:T(8,128)S(1)}, f32[32,64,128]{2,1,0:T(8,128)S(1)}, ...) custom-call(f32[64,32,1,128]{3,2,1,0:T(1,128)} %bitcast.5, f32[2,64,32,1,128]{4,3,2,1,0:T(1,128)} %bitcast.4, ...), custom_call_target="tpu_custom_call" | custom-call | tf_op jit(solution)/shard_map/propagate/pallas_call | solution.py:348
  28.6 1.5 %finish.1 = (f32[64,32,1,128]{3,2,1,0:T(1,128)}, f32[8,4,128]{2,1,0:T(4,128)}, f32[3,8,4,128]{3,2,1,0:T(4,128)}) custom-call(f32[32,64,128]{2,1,0:T(8,128)S(1)} %get-tuple-element.12.mixed, f32[32,64,128]{2,1,0:T(8,128)S(1)} %get-tuple-element.13.factor, f32[32,64,128]{2,1,0:T(8,128)S(1)} %get-tuple-element.14.total, ...), custom_call_target="tpu_custom_call" | custom-call | tf_op jit(solution)/shard_map/finish/pallas_call | solution.py:393

commit v4 on v3

--- a/solution.py
+++ b/solution.py
@@ -15,11 +15,12 @@
 Y = 4
 ROWS = X * Y
 STEPS = 2
+SIDES = [("gz", -1), ("gz", 1), ("gx", -1), ("gx", 1), ("gy", -1), ("gy", 1)]
 RATE = -0.2 / math.log(2.0)
 F32 = jnp.float32
 BF16 = jnp.bfloat16
 
-UP_X, LOW_X, UP_Y, LOW_Y, SPEED_Z, KEEP, SHAPE_0, SHAPE_1, SHAPE_2, SIGN_Z, RANK_X, RANK_Y = range(12)
+UP_X, LOW_X, UP_Y, LOW_Y, SPEED_Z, KEEP, SHAPE_0, SHAPE_1, SHAPE_2, SIGN_Z = range(10)
 
 
 def split(values):
@@ -30,11 +31,6 @@
 
 def iota(shape, dim):
     return lax.broadcasted_iota(jnp.int32, shape, dim)
-
-
-def neighbour(axis, step):
-    count = lax.axis_size(axis)
-    return {axis: lax.rem(lax.axis_index(axis) + count + step, count)}
 
 
 def stacked4(values):
@@ -111,15 +107,16 @@
 ):
     copies = []
     terms = end_terms[...]
+    for row in range(ROWS):
+        q[row] = factor[row] * whole(row, mixed, terms)
+        copy = pltpu.make_async_copy(q.at[row], out_q.at[:, row, 0, :], store_sem.at[row])
+        copy.start()
+        copies.append(copy)
     for first in range(0, ROWS, 2):
-        sums = []
-        for row in (first, first + 1):
-            value = factor[row] * whole(row, mixed, terms)
-            q[row] = value
-            copy = pltpu.make_async_copy(q.at[row], out_q.at[:, row, 0, :], store_sem.at[row])
-            copy.start()
-            copies.append(copy)
-            sums.append(jnp.concatenate(split(total[row] + forward[row] * value), axis=0))
+        sums = [
+            jnp.concatenate(split(total[row] + forward[row] * q[row]), axis=0)
+            for row in (first, first + 1)
+        ]
         sums = jnp.concatenate(sums, axis=1)
         summed = jnp.dot(
             sum4[...], jnp.concatenate([sums, sums], axis=0), preferred_element_type=F32
@@ -144,15 +141,24 @@
     q, forward_0, field, order, sphere, sign, size, weight,
     cells_0, cells_1, coef, table, mix4, pack, side4,
     send_x, send_y, send_z, recv_x, recv_y, recv_z,
-    load_sem, q_sem, forward_sem, send_sem, recv_sem,
+    load_sem, q_sem, forward_sem, send_sem, recv_sem, ready,
 ):
     forward = (forward_0, forward_1)
     grids = (cells_0, cells_1)
     barrier = pltpu.get_barrier_semaphore()
-    for axis in ("gx", "gy", "gz"):
-        for way in (1, -1):
+    here = [lax.axis_index(axis) for axis, _ in SIDES]
+    there = [
+        lax.rem(index + lax.axis_size(axis) + way, lax.axis_size(axis))
+        for index, (axis, way) in zip(here, SIDES)
+    ]
+    lower = jnp.int32(0)
+    for n, (axis, way) in enumerate(SIDES):
+        lower = lower + (there[n] < here[n]).astype(jnp.int32)
+
+        @pl.when(there[n] > here[n])
+        def _():
             pl.semaphore_signal(
-                barrier, inc=1, device_id=neighbour(axis, way), device_id_type=pl.DeviceIdType.MESH
+                barrier, inc=1, device_id={axis: there[n]}, device_id_type=pl.DeviceIdType.MESH
             )
 
     small = [
@@ -171,6 +177,19 @@
 
     lax.fori_loop(0, ROWS, load_q, 0)
 
+    @pl.when(lower > 0)
+    def _():
+        pl.semaphore_wait(barrier, lower)
+
+    for n, (axis, way) in enumerate(SIDES):
+
+        @pl.when(there[n] < here[n])
+        def _():
+            pl.semaphore_signal(
+                ready.at[n ^ 1], inc=1, device_id={axis: there[n]}, device_id_type=pl.DeviceIdType.MESH
+            )
+
+
     small[0].wait()
     small[1].wait()
     signs = sign[...].astype(F32)
@@ -179,27 +198,30 @@
     along = signed / length
     shape = along * along - 1.0 / 3.0
     speed = 0.5 * jnp.abs(along)
-    below = (iota((U, U), 0) < iota((U, U), 1)).astype(BF16)
-    ones_before = jnp.dot(signs.astype(BF16), below, preferred_element_type=F32)
-    place = iota((1, U), 1).astype(F32)
-    rank = jnp.where(signs > 0.5, ones_before, HALF + place - ones_before)
     keep = 1.0 - jnp.sum(speed, axis=0, keepdims=True)
     upper = speed * signs
     lower = speed * (1.0 - signs)
     rows = [
         upper[0:1], lower[0:1], upper[1:2], lower[1:2], speed[2:3], keep,
-        RATE * shape[0:1], RATE * shape[1:2], RATE * shape[2:3],
-        signs[2:3], rank[0:1], rank[1:2],
+        RATE * shape[0:1], RATE * shape[1:2], RATE * shape[2:3], signs[2:3],
     ]
-    stacked = jnp.zeros((16, U), F32)
     which = iota((16, U), 0)
-    for n, row in enumerate(rows):
-        stacked = jnp.where(which == n, row, stacked)
-    table[...] = jnp.zeros((LANES, LANES), F32)
-    table[0:16, 0:U] = stacked
-    columns = jnp.transpose(table[...])
-    for n in range(10):
+
+    def turned(rows):
+        stacked = jnp.zeros((16, U), F32)
+        for n, row in enumerate(rows):
+            stacked = jnp.where(which == n, row, stacked)
+        table[:, 0:U] = stacked
+        return jnp.transpose(table[...])
+
+    table[...] = jnp.zeros((16, LANES), F32)
+    columns = turned(rows)
+    for n in (SHAPE_0, SHAPE_1, SHAPE_2):
         coef[n] = jnp.broadcast_to(columns[0:U, n : n + 1], (U, LANES))
+    below = (iota((U, U), 0) < iota((U, U), 1)).astype(BF16)
+    ones_before = jnp.dot(signs.astype(BF16), below, preferred_element_type=F32)
+    place = iota((1, U), 1).astype(F32)
+    rank = jnp.where(signs > 0.5, ones_before, HALF + place - ones_before)
     for axis in range(2):
         to_rank = (iota((U, U), 0).astype(F32) == rank[axis : axis + 1]).astype(BF16)
         pack[axis] = jnp.concatenate([to_rank, to_rank], axis=1)
@@ -225,12 +247,14 @@
     for step in range(STEPS):
         cells = grids[step]
 
-        def send(n, src, dst, axis, way):
+        def send(n, src, dst):
+            axis, way = SIDES[n]
             copy = pltpu.make_async_remote_copy(
                 src_ref=src, dst_ref=dst, send_sem=send_sem.at[step, n], recv_sem=recv_sem.at[step, n],
-                device_id=neighbour(axis, way), device_id_type=pl.DeviceIdType.MESH,
-            )
-            copy.start()
+                device_id={axis: there[n]}, device_id_type=pl.DeviceIdType.MESH,
+            )
+            if step > 0:
+                copy.start()
             waits.append(copy)
             return copy
 
@@ -240,16 +264,14 @@
                 part = pl.ds(16 * group, 16)
                 for y in range(Y):
                     to = 64 * (group // 2) + 2 * (Y * x + y)
-                    turned = pltpu.roll(cells[x, y, part, :], to, 1)
+                    rolled = pltpu.roll(cells[x, y, part, :], to, 1)
                     chosen = (lane == to) | (lane == (to + 127) % 128)
-                    ends[group % 2] = jnp.where(chosen, turned, ends[group % 2])
+                    ends[group % 2] = jnp.where(chosen, rolled, ends[group % 2])
         send_z[step, 0:16, :] = ends[0]
         send_z[step, 16:32, :] = ends[1]
-        if step == 0:
-            pl.semaphore_wait(barrier, 6)
         come_z = [
-            send(0, send_z.at[step], recv_z.at[step, 0], "gz", -1),
-            send(1, send_z.at[step], recv_z.at[step, 1], "gz", 1),
+            send(0, send_z.at[step], recv_z.at[step, 0]),
+            send(1, send_z.at[step], recv_z.at[step, 1]),
         ]
         for x in range(X):
             faces = jnp.concatenate([cells[x, 0], cells[x, Y - 1]], axis=1)
@@ -259,8 +281,8 @@
             send_y[step, 0, x] = packed[0:HALF, 0:LANES]
             send_y[step, 1, x] = packed[HALF:U, LANES : 2 * LANES]
         come_y = [
-            send(2, send_y.at[step, 0], recv_y.at[step, :, 0:HALF, :], "gx", -1),
-            send(3, send_y.at[step, 1], recv_y.at[step, :, HALF:U, :], "gx", 1),
+            send(2, send_y.at[step, 0], recv_y.at[step, :, 0:HALF, :]),
+            send(3, send_y.at[step, 1], recv_y.at[step, :, HALF:U, :]),
         ]
         for y in range(Y):
             faces = jnp.concatenate([cells[0, y], cells[X - 1, y]], axis=1)
@@ -270,11 +292,33 @@
             send_x[step, 0, y] = packed[0:HALF, 0:LANES]
             send_x[step, 1, y] = packed[HALF:U, LANES : 2 * LANES]
         come_x = [
-            send(4, send_x.at[step, 0], recv_x.at[step, :, 0:HALF, :], "gy", -1),
-            send(5, send_x.at[step, 1], recv_x.at[step, :, HALF:U, :], "gy", 1),
+            send(4, send_x.at[step, 0], recv_x.at[step, :, 0:HALF, :]),
+            send(5, send_x.at[step, 1], recv_x.at[step, :, HALF:U, :]),
         ]
 
         if step == 0:
+            far = [
+                (there[n] > here[n] + 1) | ((there[n] == 2) if axis == "gz" else False)
+                for n, (axis, way) in enumerate(SIDES)
+            ]
+            for n in range(6):
+                pl.when(there[n] < here[n])(waits[n].start)
+
+            def meet(n):
+                pl.semaphore_wait(ready.at[n], 1)
+                waits[n].start()
+
+            for n in (1, 5, 3, 0, 4, 2):
+                pl.when((there[n] > here[n]) & ~far[n])(functools.partial(meet, n))
+            for n in (1, 0, 5, 4, 3, 2):
+                pl.when((there[n] > here[n]) & far[n])(functools.partial(meet, n))
+
+        if step == 0:
+            for n in range(10):
+                if n not in (SHAPE_0, SHAPE_1, SHAPE_2):
+                    coef[n] = jnp.broadcast_to(columns[0:U, n : n + 1], (U, LANES))
+            ranks = turned([rank[0:1], rank[1:2]])
+
             def load_forward(row, carry):
                 for n in range(STEPS):
                     pltpu.make_async_copy(
@@ -296,7 +340,7 @@
             high, low = split(sphere[...])
             mix4[...] = jnp.concatenate([high, high, low, low], axis=1)
             for axis in range(2):
-                of_rank = columns[0:U, RANK_X + axis : RANK_X + axis + 1]
+                of_rank = ranks[0:U, axis : axis + 1]
                 from_rank = (iota((U, U), 1).astype(F32) == of_rank).astype(BF16)
                 high, low = split(sphere[...] * speed[axis : axis + 1])
                 sorted_mix = jnp.dot(
@@ -364,7 +408,7 @@
             pltpu.VMEM((X, Y, U, LANES), F32),
             pltpu.VMEM((X, Y, U, LANES), F32),
             pltpu.VMEM((10, U, LANES), F32),
-            pltpu.VMEM((LANES, LANES), F32),
+            pltpu.VMEM((16, LANES), F32),
             pltpu.VMEM((U, 4 * U), BF16),
             pltpu.VMEM((2, U, 2 * U), BF16),
             pltpu.VMEM((2, 2, U, LANES), BF16),
@@ -379,6 +423,7 @@
             pltpu.SemaphoreType.DMA((STEPS,)),
             pltpu.SemaphoreType.DMA((STEPS, 6)),
             pltpu.SemaphoreType.DMA((STEPS, 6)),
+            pltpu.SemaphoreType.REGULAR((6,)),
         ],
         compiler_params=pltpu.CompilerParams(
             collective_id=0, has_side_effects=True, vmem_limit_bytes=32 * 1024 * 1024

time: 30.4 us -> 29 us (0.954)
  the two profiles are of different devices: /device:TPU:1 before, /device:TPU:48 now
where the time goes in v4:
time: 29 us; the launch traced here: 28.6 us
  Pallas kernels  28 us (97%)
  between operations  0.64 us (2%)
    pallas_call x1, Pallas kernels, body(): pl.pallas_call(kernel, out_shape=(block, block, block, block, pltpu.VMEM(...  26.5 us
    pallas_call x1, Pallas kernels, body(): pl.pallas_call(finish, out_shape=(jax.ShapeDtypeStruct(cells, F32), jax.S...  1.49 us

profile of v4, /device:TPU:48, one launch (start us, length us, event | category | flops | bytes accessed | tf_op | source)
XLA Modules:
  0.0 28.6 jit_solution(9219259393338180142)
XLA Ops:
  0.6 26.5 %propagate.1 = (f32[32,64,128]{2,1,0:T(8,128)S(1)}, f32[32,64,128]{2,1,0:T(8,128)S(1)}, f32[32,64,128]{2,1,0:T(8,128)S(1)}, f32[32,64,128]{2,1,0:T(8,128)S(1)}, ...) custom-call(f32[64,32,1,128]{3,2,1,0:T(1,128)} %bitcast.5, f32[2,64,32,1,128]{4,3,2,1,0:T(1,128)} %bitcast.4, ...), custom_call_target="tpu_custom_call" | custom-call | tf_op jit(solution)/shard_map/propagate/pallas_call | solution.py:392
  27.1 1.5 %finish.1 = (f32[64,32,1,128]{3,2,1,0:T(1,128)}, f32[8,4,128]{2,1,0:T(4,128)}, f32[3,8,4,128]{3,2,1,0:T(4,128)}) custom-call(f32[32,64,128]{2,1,0:T(8,128)S(1)} %get-tuple-element.12.mixed, f32[32,64,128]{2,1,0:T(8,128)S(1)} %get-tuple-element.13.factor, f32[32,64,128]{2,1,0:T(8,128)S(1)} %get-tuple-element.14.total, ...), custom_call_target="tpu_custom_call" | custom-call | tf_op jit(solution)/shard_map/finish/pallas_call | solution.py:438

commit v5 on v4

--- a/solution.py
+++ b/solution.py
@@ -243,7 +243,7 @@
                 factor[Y * x + y, part, :] = value
                 cells_0[x, y, part, :] = value * q[Y * x + y, part, :]
 
-    waits = []
+    waits = {}
     for step in range(STEPS):
         cells = grids[step]
 
@@ -255,9 +255,20 @@
             )
             if step > 0:
                 copy.start()
-            waits.append(copy)
+            waits[step, n] = copy
             return copy
 
+        for x in range(X):
+            faces = jnp.concatenate([cells[x, 0], cells[x, Y - 1]], axis=1)
+            packed = jnp.dot(
+                pack[1], jnp.concatenate(split(faces), axis=0), preferred_element_type=F32
+            )
+            send_y[step, 0, x] = packed[0:HALF, 0:LANES]
+            send_y[step, 1, x] = packed[HALF:U, LANES : 2 * LANES]
+        come_y = [
+            send(2, send_y.at[step, 0], recv_y.at[step, :, 0:HALF, :]),
+            send(3, send_y.at[step, 1], recv_y.at[step, :, HALF:U, :]),
+        ]
         ends = [jnp.zeros((16, LANES), F32)] * 2
         for x in range(X):
             for group in range(4):
@@ -273,17 +284,6 @@
             send(0, send_z.at[step], recv_z.at[step, 0]),
             send(1, send_z.at[step], recv_z.at[step, 1]),
         ]
-        for x in range(X):
-            faces = jnp.concatenate([cells[x, 0], cells[x, Y - 1]], axis=1)
-            packed = jnp.dot(
-                pack[1], jnp.concatenate(split(faces), axis=0), preferred_element_type=F32
-            )
-            send_y[step, 0, x] = packed[0:HALF, 0:LANES]
-            send_y[step, 1, x] = packed[HALF:U, LANES : 2 * LANES]
-        come_y = [
-            send(2, send_y.at[step, 0], recv_y.at[step, :, 0:HALF, :]),
-            send(3, send_y.at[step, 1], recv_y.at[step, :, HALF:U, :]),
-        ]
         for y in range(Y):
             faces = jnp.concatenate([cells[0, y], cells[X - 1, y]], axis=1)
             packed = jnp.dot(
@@ -302,11 +302,11 @@
                 for n, (axis, way) in enumerate(SIDES)
             ]
             for n in range(6):
-                pl.when(there[n] < here[n])(waits[n].start)
+                pl.when(there[n] < here[n])(waits[0, n].start)
 
             def meet(n):
                 pl.semaphore_wait(ready.at[n], 1)
-                waits[n].start()
+                waits[0, n].start()
 
             for n in (1, 5, 3, 0, 4, 2):
                 pl.when((there[n] > here[n]) & ~far[n])(functools.partial(meet, n))
@@ -367,6 +367,15 @@
             recv_x.at[step], side4.at[0], mixed,
             [[Y * (X - 1) + y for y in range(Y)], list(range(Y))],
         )
+        def close(ys):
+            for row in range(ROWS):
+                if row % Y in ys:
+                    value = factor[row] * whole(row, mixed, terms)
+                    cells_1[row // Y, row % Y] = factor[row] * value
+                    total[row] = forward_0[row] * value
+
+        if step == 0:
+            close((1, 2))
         for copy in come_y:
             copy.wait_recv()
         add_sides(
@@ -374,13 +383,10 @@
             [[Y * x + Y - 1 for x in range(X)], [Y * x for x in range(X)]],
         )
         if step == 0:
-            for row in range(ROWS):
-                value = factor[row] * whole(row, mixed, terms)
-                cells_1[row // Y, row % Y] = factor[row] * value
-                total[row] = forward_0[row] * value
+            close((0, Y - 1))
         else:
             terms_out[...] = terms
-    for copy in waits:
+    for copy in waits.values():
         copy.wait_send()
 
 

time: 29 us -> 28.7 us (0.990)
  Pallas kernels: 28 us -> 27.7 us
where the time goes in v5:
time: 28.7 us; the launch traced here: 28.3 us
  Pallas kernels  27.7 us (97%)
  between operations  0.64 us (2%)
    pallas_call x1, Pallas kernels, body(): pl.pallas_call(kernel, out_shape=(block, block, block, block, pltpu.VMEM(...  26.2 us
    pallas_call x1, Pallas kernels, body(): pl.pallas_call(finish, out_shape=(jax.ShapeDtypeStruct(cells, F32), jax.S...  1.49 us

profile of v5, /device:TPU:48, one launch (start us, length us, event | category | flops | bytes accessed | tf_op | source)
XLA Modules:
  0.0 28.3 jit_solution(8749949371964027222)
XLA Ops:
  0.6 26.2 %propagate.1 = (f32[32,64,128]{2,1,0:T(8,128)S(1)}, f32[32,64,128]{2,1,0:T(8,128)S(1)}, f32[32,64,128]{2,1,0:T(8,128)S(1)}, f32[32,64,128]{2,1,0:T(8,128)S(1)}, ...) custom-call(f32[64,32,1,128]{3,2,1,0:T(1,128)} %bitcast.5, f32[2,64,32,1,128]{4,3,2,1,0:T(1,128)} %bitcast.4, ...), custom_call_target="tpu_custom_call" | custom-call | tf_op jit(solution)/shard_map/propagate/pallas_call | solution.py:398
  26.8 1.5 %finish.1 = (f32[64,32,1,128]{3,2,1,0:T(1,128)}, f32[8,4,128]{2,1,0:T(4,128)}, f32[3,8,4,128]{3,2,1,0:T(4,128)}) custom-call(f32[32,64,128]{2,1,0:T(8,128)S(1)} %get-tuple-element.12.mixed, f32[32,64,128]{2,1,0:T(8,128)S(1)} %get-tuple-element.13.factor, f32[32,64,128]{2,1,0:T(8,128)S(1)} %get-tuple-element.14.total, ...), custom_call_target="tpu_custom_call" | custom-call | tf_op jit(solution)/shard_map/finish/pallas_call | solution.py:444

commit v6 on v5

--- a/solution.py
+++ b/solution.py
@@ -85,8 +85,8 @@
     return jnp.dot(mix4[...], stacked4(ends), preferred_element_type=F32)
 
 
-def add_sides(recv, side4, mixed, rows):
-    for way in range(2):
+def add_sides(recv, side4, mixed, rows, ways=(0, 1)):
+    for way in ways:
         part = pl.ds(HALF * way, HALF)
         for place in range(0, len(rows[way]), 2):
             pair = jnp.concatenate([recv[place, part, :], recv[place + 1, part, :]], axis=1)
@@ -376,14 +376,14 @@
 
         if step == 0:
             close((1, 2))
-        for copy in come_y:
+        for way, copy in enumerate(come_y):
             copy.wait_recv()
-        add_sides(
-            recv_y.at[step], side4.at[1], mixed,
-            [[Y * x + Y - 1 for x in range(X)], [Y * x for x in range(X)]],
-        )
-        if step == 0:
-            close((0, Y - 1))
+            add_sides(
+                recv_y.at[step], side4.at[1], mixed,
+                [[Y * x + Y - 1 for x in range(X)], [Y * x for x in range(X)]], (way,),
+            )
+            if step == 0:
+                close((Y - 1,) if way == 0 else (0,))
         else:
             terms_out[...] = terms
     for copy in waits.values():

time: 28.7 us -> 28.7 us (level)
  no operation moved by 1% of the time
where the time goes in v6:
time: 28.7 us; the launch traced here: 28.4 us
  Pallas kernels  27.7 us (97%)
  between operations  0.64 us (2%)
    pallas_call x1, Pallas kernels, body(): pl.pallas_call(kernel, out_shape=(block, block, block, block, pltpu.VMEM(...  26.2 us
    pallas_call x1, Pallas kernels, body(): pl.pallas_call(finish, out_shape=(jax.ShapeDtypeStruct(cells, F32), jax.S...  1.49 us

profile of v6, /device:TPU:48, one launch (start us, length us, event | category | flops | bytes accessed | tf_op | source)
XLA Modules:
  0.0 28.4 jit_solution(1709926927708222738)
XLA Ops:
  0.6 26.2 %propagate.1 = (f32[32,64,128]{2,1,0:T(8,128)S(1)}, f32[32,64,128]{2,1,0:T(8,128)S(1)}, f32[32,64,128]{2,1,0:T(8,128)S(1)}, f32[32,64,128]{2,1,0:T(8,128)S(1)}, ...) custom-call(f32[64,32,1,128]{3,2,1,0:T(1,128)} %bitcast.5, f32[2,64,32,1,128]{4,3,2,1,0:T(1,128)} %bitcast.4, ...), custom_call_target="tpu_custom_call" | custom-call | tf_op jit(solution)/shard_map/propagate/pallas_call | solution.py:398
  26.9 1.5 %finish.1 = (f32[64,32,1,128]{3,2,1,0:T(1,128)}, f32[8,4,128]{2,1,0:T(4,128)}, f32[3,8,4,128]{3,2,1,0:T(4,128)}) custom-call(f32[32,64,128]{2,1,0:T(8,128)S(1)} %get-tuple-element.12.mixed, f32[32,64,128]{2,1,0:T(8,128)S(1)} %get-tuple-element.13.factor, f32[32,64,128]{2,1,0:T(8,128)S(1)} %get-tuple-element.14.total, ...), custom_call_target="tpu_custom_call" | custom-call | tf_op jit(solution)/shard_map/finish/pallas_call | solution.py:444
